TPU v7x, 128 devices: a whole 4x4x4 slice. The times are simulated.
128 devices in a mesh: node: 8 (over z_lo, y), local: 16 (over x, z_hi, core).
Axes of the slice: x: 4, y: 4, z: 4 (z_hi: 2, z_lo: 2; z = z_hi * 2 + z_lo), core: 2. Of those that a mesh axis runs over, the one named last changes fastest.
Arguments:
- cache_pool: bfloat16 [512, 576, 256], P(('node', 'local')), may hold values from -6 to 6
- block_table: int32 [256, 2], P(('node', 'local')), may hold values from 0 to 3, as said below
- lengths: int32 [256], replicated, may hold values from 128 to 512
- mig_slot: int32 [128], replicated, may hold values from 0 to 1
- mig_dest: int32 [128], replicated, may hold values from 0 to 127, each once
- queries: bfloat16 [3, 256, 73728], P(None, ('node', 'local'))
- new_entries: bfloat16 [3, 256, 576], P(None, ('node', 'local')), may hold values from -6 to 6
- residual: bfloat16 [3, 256, 7168], P(None, None, 'node'), may hold values from -0.75 to 0.75
- w_uv: bfloat16 [128, 512, 128], P('local'), may hold values from -0.25 to 0.25
- w_out: bfloat16 [16384, 7168], P('local', 'node'), may hold values from -0.046875 to 0.046875
- norm_gain: float32 [7168], P('node'), may hold values from 0.1 to 1.9
- w_gate: bfloat16 [7168, 18432], P('node', 'local'), may hold values from -0.0625 to 0.0625
- w_up: bfloat16 [7168, 18432], P('node', 'local'), may hold values from -0.0625 to 0.0625
- w_down: bfloat16 [18432, 7168], P('local', 'node'), may hold values from -0.046875 to 0.046875
Outputs:
- layer_out: bfloat16 [3, 256, 7168], P(None, 'local', 'node')
Inputs may be any that keep to these rules, and one draw needn't show every extreme that they name: `block_table`: the 2 rows of one device name each of its 4 pool blocks once. `mig_dest`: every device is the destination of exactly one device, possibly itself.
All inputs are finite; a program needn't handle non-finite values.
Results may differ from a plain program's by a relative error of at most 0.035.
Values may be sent and summed in bfloat16 or wider, within the bound.
A program may use at most 128 MiB of HBM per device.

v0:
```python
import jax
import jax.numpy as jnp
from jax import lax
from jax.sharding import PartitionSpec as P

D = 7168
LATENT = 512
ROPE = 64
QK_NOPE = 128


epsilon = 1e-06


def attend(queries_now, caches, lengths_now, fresh_keys, score_scale):
    blocks = caches.shape[1]
    columns = caches.shape[3]
    scores = (
        jnp.einsum("rhc,rbct->rhbt", queries_now, caches, preferred_element_type=jnp.float32)
        * score_scale
    )
    position = lax.broadcasted_iota(
        jnp.int32, (blocks, columns), 0
    ) * columns + lax.broadcasted_iota(jnp.int32, (blocks, columns), 1)
    visible = position[None, :, :] < lengths_now[:, None, None]
    scores = jnp.where(visible[:, None, :, :], scores, -jnp.inf)
    fresh_scores = (
        jnp.einsum("rhc,nrc->rhn", queries_now, fresh_keys, preferred_element_type=jnp.float32)
        * score_scale
    )
    highest = jnp.maximum(jnp.max(scores, axis=(2, 3)), jnp.max(fresh_scores, axis=2))
    cache_weights = jnp.exp(scores - highest[:, :, None, None])
    fresh_weights = jnp.exp(fresh_scores - highest[:, :, None])
    totals = jnp.sum(cache_weights, axis=(2, 3)) + jnp.sum(fresh_weights, axis=2)
    cache_weights = (cache_weights / totals[:, :, None, None]).astype(jnp.bfloat16)
    fresh_weights = (fresh_weights / totals[:, :, None]).astype(jnp.bfloat16)
    context = jnp.einsum(
        "rhbt,rbct->rhc",
        cache_weights,
        caches[:, :, :LATENT, :],
        preferred_element_type=jnp.float32,
    )
    context = context + jnp.einsum(
        "rhn,nrc->rhc", fresh_weights, fresh_keys[:, :, :LATENT], preferred_element_type=jnp.float32
    )
    return context.astype(jnp.bfloat16)


def forward_pick(landed, aims, usable, peers):
    matches = (aims[None, :] == jnp.arange(peers, dtype=jnp.int32)[:, None]) & usable[None, :]
    chosen = jnp.argmax(matches, axis=1)
    present = jnp.any(matches, axis=1)
    return jnp.where(present[:, None, None, None], landed[chosen], jnp.zeros((), landed.dtype))


def local(
    cache_pool,
    block_table,
    lengths,
    mig_slot,
    mig_dest,
    queries,
    new_entries,
    residual,
    w_uv,
    w_out,
    norm_gain,
    w_gate,
    w_up,
    w_down,
):
    req_dev = block_table.shape[0]
    steps_total = queries.shape[0]
    n_node = lax.axis_size("node")
    n_local = lax.axis_size("local")
    node_index = lax.axis_index("node")
    local_index = lax.axis_index("local")
    self_index = node_index * n_local + local_index
    score_scale = (QK_NOPE + ROPE) ** (-0.5)
    heads_total = w_uv.shape[0] * n_local
    caches = cache_pool[block_table]
    leave_slot = mig_slot[self_index]
    target = mig_dest[self_index]
    anchor = jnp.argmax(mig_dest == self_index)
    leaving = lax.dynamic_index_in_dim(caches, leave_slot, 0, keepdims=False)
    own_lengths = lax.dynamic_slice_in_dim(lengths, self_index * req_dev, req_dev)
    arrival_length = lengths[anchor * req_dev + mig_slot[anchor]]
    is_leaving = jnp.arange(req_dev, dtype=jnp.int32) == leave_slot
    serve_lengths = jnp.where(is_leaving, arrival_length, own_lengths)
    step_queries = queries.reshape(steps_total, req_dev, heads_total, -1)
    empty_block = jnp.zeros((), leaving.dtype)
    picks = jnp.arange(n_node, dtype=jnp.int32) == target // n_local
    outbound = jnp.where(picks[:, None, None, None], leaving[None], empty_block)
    landed = lax.all_to_all(outbound, "node", split_axis=0, concat_axis=0, tiled=True)
    senders = jnp.arange(n_node, dtype=jnp.int32) * n_local + local_index
    aims = mig_dest[senders]
    onward = forward_pick(landed, aims % n_local, aims // n_local == node_index, n_local)
    arrived = lax.all_to_all(onward, "local", split_axis=0, concat_axis=0, tiled=True)
    arrival = lax.dynamic_index_in_dim(arrived, anchor % n_local, 0, keepdims=False)
    serving = jnp.where(is_leaving[:, None, None, None], arrival[None], caches)
    contexts = [
        attend(
            step_queries[step_index],
            serving,
            serve_lengths,
            new_entries[: step_index + 1],
            score_scale,
        )
        for step_index in range(steps_total)
    ]
    outputs = []
    for step_index in range(steps_total):
        grouped = lax.all_to_all(
            contexts[step_index], "local", split_axis=1, concat_axis=0, tiled=True
        )
        values = jnp.einsum(
            "rhc,hcv->rhv", grouped, w_uv, preferred_element_type=jnp.float32
        ).astype(jnp.bfloat16)
        values = values.reshape(values.shape[0], -1)
        partial_value = jnp.dot(
            lax.all_gather(values, "node", axis=0, tiled=True),
            w_out,
            preferred_element_type=jnp.float32,
        )
        attn_out = lax.psum(partial_value.astype(jnp.bfloat16), "local").astype(jnp.float32)
        mixed = (residual[step_index].astype(jnp.float32) + attn_out).astype(jnp.bfloat16)
        mixed_wide = mixed.astype(jnp.float32)
        squares = lax.psum(jnp.sum(mixed_wide * mixed_wide, axis=1), "node")
        inverse = lax.rsqrt(squares / D + epsilon)
        normed = (mixed_wide * inverse[:, None] * norm_gain[None, :]).astype(jnp.bfloat16)
        gate_part = jnp.dot(normed, w_gate, preferred_element_type=jnp.float32)
        up_part = jnp.dot(normed, w_up, preferred_element_type=jnp.float32)
        gate, upward = (
            lax.psum(gate_part.astype(jnp.bfloat16), "node").astype(jnp.float32),
            lax.psum(up_part.astype(jnp.bfloat16), "node").astype(jnp.float32),
        )
        hidden = (jax.nn.silu(gate) * upward).astype(jnp.bfloat16)
        share_rows = hidden.shape[0] // n_local
        block_out = lax.psum_scatter(
            jnp.dot(hidden, w_down, preferred_element_type=jnp.float32).astype(jnp.bfloat16),
            "local",
            scatter_dimension=0,
            tiled=True,
        ).astype(jnp.float32)
        base_rows = lax.dynamic_slice_in_dim(mixed_wide, local_index * share_rows, share_rows, 0)
        outputs.append((base_rows + block_out).astype(jnp.bfloat16))
    return jnp.stack(outputs)


def solution(mesh):
    in_specs = (
        P(("node", "local"), None, None),
        P(("node", "local"), None),
        P(),
        P(),
        P(),
        P(None, ("node", "local"), None),
        P(None, ("node", "local"), None),
        P(None, None, "node"),
        P("local", None, None),
        P("local", "node"),
        P("node"),
        P("node", "local"),
        P("node", "local"),
        P("local", "node"),
    )
    out_specs = P(None, "local", "node")
    return jax.shard_map(local, mesh=mesh, in_specs=in_specs, out_specs=out_specs, check_vma=False)
```

profile of v0, /device:TPU:1, one launch (start us, length us, event | category | flops | bytes accessed | tf_op | source)
XLA Modules:
  0.0 886.0 jit_solution(14766332666660187852)
XLA Ops:
  6.5 1.5 dynamic_slice.36
  10.1 1.4 compare_reduce_fusion
  14.3 1.3 fusion.86
  18.3 1.9 gather_fusion.1
  20.2 2.6 broadcast_select_fusion.1
  22.9 6.5 all-to-all-start
  30.9 53.8 %all-to-all-done = bf16[8,2,576,256]{3,2,1,0:T(8,128)(2,1)} async-done(((bf16[8,2,576,256]{3,2,1,0:T(8,128)(2,1)}), bf16[8,2,576,256]{3,2,1,0:T(8,128)(2,1)}, u32[]{:S(2)}, u32[]{:S(2)}) %all-to-all-start) | async-done | bytes 4718624 | tf_op jit(solution)/shard_map/all_to_all | solution.py:94
  84.6 7.3 gather_fusion.2
  91.9 8.0 broadcast_select_fusion
  100.0 8.2 all-to-all-start.1
  108.1 2.6 fusion.85
  113.5 2.0 squeeze.34
  116.2 2.0 squeeze.33
  118.2 1.1 squeeze.32
  120.5 1.4 dynamic-slice_select_fusion
  123.4 1.2 fusion.60
  124.6 1.2 fusion.89
  125.8 1.2 fusion.91
  127.0 130.4 %all-to-all-done.1 = bf16[16,2,576,256]{3,2,1,0:T(8,128)(2,1)} async-done(((bf16[16,2,576,256]{3,2,1,0:T(8,128)(2,1)}), bf16[16,2,576,256]{3,2,1,0:T(8,128)(2,1)}, u32[]{:S(2)}, u32[]{:S(2)}) %all-to-all-start.1) | async-done | bytes 9437216 | tf_op jit(solution)/shard_map/all_to_all | solution.py:98
  257.4 1.1 dynamic-slice_bitcast_fusion
  258.7 0.7 copy-done.6
  260.6 1.5 fusion.88
  262.1 1.5 fusion.87
  264.6 1.0 copy.82
  265.5 8.2 all-to-all-start.4
  273.7 1.1 fusion.41
  274.9 1.5 convolution_bitcast_fusion.1
  276.7 1.0 copy.74
  278.3 1.0 copy.66
  279.3 3.3 all-to-all-done.4
  282.6 4.3 all-to-all-start.3
  286.9 0.9 copy.119
  287.8 1.1 all_to_all.58
  289.2 38.7 %all_gather.11 = bf16[256,1024]{1,0:T(8,128)(2,1)} all-gather(bf16[32,1024]{1,0:T(8,128)(2,1)S(1)} %bitcast.168), channel_id=1, replica_groups=mesh['node'=8,'local'=16] {'node'}, dimensions={0}, use_global_device_ids=true | all-gather | bytes 589824 | tf_op jit(solution)/shard_map/all_gather | solution.py:121
  327.9 13.7 %all-to-all-start.2 = ((bf16[2,128,512]{2,0,1:T(2,128)(2,1)}), bf16[2,128,512]{2,0,1:T(2,128)(2,1)S(1)}, u32[]{:S(2)}, u32[]{:S(2)}) async-start(bf16[2,128,512]{2,0,1:T(2,128)(2,1)} %copy.66), calls=%async_computation.2 | async-start | bytes 524288 | tf_op jit(solution)/shard_map/all_to_all | solution.py:113
  341.6 1.8 copy.120
  343.5 1.8 all_to_all.54
  345.2 1.3 fusion.26
  346.5 23.5 %all_gather.10 = bf16[256,1024]{1,0:T(8,128)(2,1)S(1)} all-gather(bf16[32,1024]{1,0:T(8,128)(2,1)S(1)} %bitcast.169), channel_id=1, replica_groups=mesh['node'=8,'local'=16] {'node'}, dimensions={0}, use_global_device_ids=true | all-gather | bytes 589824 | tf_op jit(solution)/shard_map/all_gather | solution.py:121
  370.0 3.1 convolution_convert_fusion.9
  373.1 1.5 convolution_convert_fusion.10
  374.6 0.9 copy.121
  375.5 1.1 all_to_all.50
  376.9 23.4 %all_gather.9 = bf16[256,1024]{1,0:T(8,128)(2,1)S(1)} all-gather(bf16[32,1024]{1,0:T(8,128)(2,1)S(1)} %bitcast.170), channel_id=1, replica_groups=mesh['node'=8,'local'=16] {'node'}, dimensions={0}, use_global_device_ids=true | all-gather | bytes 589824 | tf_op jit(solution)/shard_map/all_gather | solution.py:121
  400.3 1.5 convolution_convert_fusion.11
  401.8 154.5 %all-reduce.6.cloned.1.call-done = (bf16[256,896]{1,0:T(8,128)(2,1)}, bf16[256,896]{1,0:T(8,128)(2,1)}, bf16[256,896]{1,0:T(8,128)(2,1)}) async-done(((bf16[256,896]{1,0:T(8,128)(2,1)}, bf16[256,896]{1,0:T(8,128)(2,1)}, bf16[256,896]{1,0:T(8,128)(2,1)}), (bf16[256,896]{1,0:T(8,128)(2,1)}, bf16[256,896]{1,0:T(8,128)(2,1)}, bf16[256,896]{1,0:T(8,128)(2,1)})) %all-reduce.6.cloned.1.call-update) | async-done | bytes 1376272 | tf_op jit(solution)/shard_map/psum | solution.py:125
  556.3 3.0 multiply_reduce_fusion.2
  559.3 14.9 %all-reduce = (f32[256]{0:T(256)S(1)}, f32[256]{0:T(256)S(1)}, f32[256]{0:T(256)S(1)}) all-reduce(f32[256]{0:T(256)S(1)} %get-tuple-element.11, f32[256]{0:T(256)S(1)} %get-tuple-element.10, f32[256]{0:T(256)S(1)} %get-tuple-element.9), channel_id=1, replica_groups=mesh['node'=8,'local'=16] {'node'}, use_global_device_ids=true, to_apply=%region_27.28 | all-reduce | flops 768 | bytes 6144 | tf_op jit(solution)/shard_map/psum | solution.py:128
  574.2 2.9 convolution_convert_fusion.5
  577.1 1.7 convolution_convert_fusion.4
  578.8 1.8 convolution_convert_fusion.3
  580.6 1.7 convolution_convert_fusion.2
  582.4 1.7 convolution_convert_fusion.1
  584.1 1.8 convolution_convert_fusion
  586.0 96.1 %all-reduce.8.cloned.1.call-done = (bf16[256,1152]{1,0:T(8,128)(2,1)}, bf16[256,1152]{1,0:T(8,128)(2,1)}, bf16[256,1152]{1,0:T(8,128)(2,1)}, bf16[256,1152]{1,0:...) async-done(((bf16[256,1152]{1,0:T(8,128)(2,1)}, bf16[256,1152]{1,0:T(8,128)(2,1)}, bf16[256,1152]{1,0:T(8,128)(2,1)}, bf16[256,1152]{1,0:T(8,128)(2,1)}, ...) | async-done | bytes 3538960 | tf_op jit(solution)/shard_map/psum | solution.py:135
  682.0 3.6 convolution_convert_fusion.8
  685.7 3.7 convolution_convert_fusion.7
  689.5 3.2 convolution_convert_fusion.6
  692.8 53.6 %reduce-scatter.4.cloned.1.call-done = bf16[16,896]{1,0:T(8,128)(2,1)} async-done(((bf16[256,896]{1,0:T(8,128)(2,1)}), bf16[16,896]{1,0:T(8,128)(2,1)}) %reduce-scatter.4.cloned.1.call-update) | async-done | bytes 28688 | tf_op jit(solution)/shard_map/reduce_scatter | solution.py:139
  746.4 0.8 fusion.55
  747.3 64.7 %reduce-scatter.6.cloned.1.call-done = bf16[16,896]{1,0:T(8,128)(2,1)} async-done(((bf16[256,896]{1,0:T(8,128)(2,1)}), bf16[16,896]{1,0:T(8,128)(2,1)}) %reduce-scatter.6.cloned.1.call-update) | async-done | bytes 28688 | tf_op jit(solution)/shard_map/reduce_scatter | solution.py:139
  812.0 0.8 fusion.56
  812.8 65.1 %reduce-scatter.8.cloned.1.call-done = bf16[16,896]{1,0:T(8,128)(2,1)} async-done(((bf16[256,896]{1,0:T(8,128)(2,1)}), bf16[16,896]{1,0:T(8,128)(2,1)}) %reduce-scatter.8.cloned.1.call-update) | async-done | bytes 28688 | tf_op jit(solution)/shard_map/reduce_scatter | solution.py:139
  878.0 0.8 fusion.57
  (99 shorter events, 10.6 us)
Async XLA Ops:
  6.5 567.6 %copy-start = (bf16[896,1152]{1,0:T(8,128)(2,1)S(1)}, bf16[896,1152]{1,0:T(8,128)(2,1)}, u32[]{:S(2)}) copy-start(bf16[896,1152]{1,0:T(8,128)(2,1)} %param.25) | copy-start | bytes 6193156
  22.9 6.5 copy-start.1
  22.9 61.7 %all-to-all-start = ((bf16[8,2,576,256]{3,2,1,0:T(8,128)(2,1)}), bf16[8,2,576,256]{3,2,1,0:T(8,128)(2,1)}, u32[]{:S(2)}, u32[]{:S(2)}) async-start(bf16[8,2,576,256]{3,2,1,0:T(8,128)(2,1)} %broadcast_select_fusion.1), calls=%async_computation | async-start | bytes 9437184 | tf_op jit(solution)/shard_map/all_to_all | solution.py:94
  100.0 157.4 %all-to-all-start.1 = ((bf16[16,2,576,256]{3,2,1,0:T(8,128)(2,1)}), bf16[16,2,576,256]{3,2,1,0:T(8,128)(2,1)}, u32[]{:S(2)}, u32[]{:S(2)}) async-start(bf16[16,2,576,256]{3,2,1,0:T(8,128)(2,1)} %broadcast_select_fusion), calls=%async_computation.1 | async-start | bytes 18874368 | tf_op jit(solution)/shard_map/all_to_all | solution.py:98
  110.7 8.6 copy-start.14
  258.5 1.0 copy-start.6
  259.4 4.3 copy-start.7
  259.4 1.2 copy-start.5
  260.6 1.5 copy-start.4
  264.3 10.6 %copy-start.8 = (bf16[2,2,576,256]{3,2,1,0:T(8,128)(2,1)S(1)}, bf16[2,2,576,256]{3,2,1,0:T(8,128)(2,1)}, u32[]{:S(2)}) copy-start(bf16[2,2,576,256]{3,2,1,0:T(8,128)(2,1)} %copy-done.7) | copy-start | bytes 3538948
  265.5 17.1 %all-to-all-start.4 = ((bf16[2,128,512]{2,0,1:T(2,128)(2,1)}), bf16[2,128,512]{2,0,1:T(2,128)(2,1)S(1)}, u32[]{:S(2)}, u32[]{:S(2)}) async-start(bf16[2,128,512]{2,0,1:T(2,128)(2,1)} %copy.82), calls=%async_computation.6 | async-start | bytes 524288 | tf_op jit(solution)/shard_map/all_to_all | solution.py:113
  276.4 1.3 copy-start.10
  278.3 10.6 %copy-start.2 = (bf16[8,512,128]{2,1,0:T(8,128)(2,1)S(1)}, bf16[8,512,128]{2,1,0:T(8,128)(2,1)}, u32[]{:S(2)}) copy-start(bf16[8,512,128]{2,1,0:T(8,128)(2,1)} %param.22) | copy-start | bytes 3145732
  282.6 45.3 %all-to-all-start.3 = ((bf16[2,128,512]{2,0,1:T(2,128)(2,1)}), bf16[2,128,512]{2,0,1:T(2,128)(2,1)}, u32[]{:S(2)}, u32[]{:S(2)}) async-start(bf16[2,128,512]{2,0,1:T(2,128)(2,1)} %copy.74), calls=%async_computation.4 | async-start | bytes 524288 | tf_op jit(solution)/shard_map/all_to_all | solution.py:113
  327.9 46.7 %all-to-all-start.2 = ((bf16[2,128,512]{2,0,1:T(2,128)(2,1)}), bf16[2,128,512]{2,0,1:T(2,128)(2,1)S(1)}, u32[]{:S(2)}, u32[]{:S(2)}) async-start(bf16[2,128,512]{2,0,1:T(2,128)(2,1)} %copy.66), calls=%async_computation.2 | async-start | bytes 524288 | tf_op jit(solution)/shard_map/all_to_all | solution.py:113
  341.6 214.7 %all-reduce.6.cloned.1.call-start = ((), (), s32[]{:S(2)}) async-start(), calls=%async_computation.11 | async-start | bytes 2752512 | tf_op jit(solution)/shard_map/psum | solution.py:125
  345.2 24.8 %copy-start.9 = (bf16[256,1024]{1,0:T(8,128)(2,1)S(1)}, bf16[256,1024]{1,0:T(8,128)(2,1)}, u32[]{:S(2)}) copy-start(bf16[256,1024]{1,0:T(8,128)(2,1)} %all_gather.11) | copy-start | bytes 1572868
  370.0 3.1 copy-start.16
  376.5 23.7 %copy-start.17 = (bf16[1024,896]{1,0:T(8,128)(2,1)S(1)}, bf16[1024,896]{1,0:T(8,128)(2,1)}, u32[]{:S(2)}) copy-start(bf16[1024,896]{1,0:T(8,128)(2,1)} %param.23) | copy-start | bytes 5505028
  401.7 154.5 %copy-start.3 = (bf16[3,256,896]{2,1,0:T(8,128)(2,1)S(1)}, bf16[3,256,896]{2,1,0:T(8,128)(2,1)}, u32[]{:S(2)}) copy-start(bf16[3,256,896]{2,1,0:T(8,128)(2,1)} %param.21) | copy-start | bytes 4128772
  401.8 280.3 %all-reduce.8.cloned.1.call-start = ((), (), s32[]{:S(2)}) async-start(), calls=%async_computation.12 | async-start | bytes 7077888 | tf_op jit(solution)/shard_map/psum | solution.py:135
  556.3 17.9 %copy-start.20 = (f32[896]{0:T(1024)S(1)}, f32[896]{0:T(1024)}, u32[]{:S(2)}) copy-start(f32[896]{0:T(1024)} %param.24) | copy-start | bytes 10756
  574.2 2.9 copy-start.13
  574.2 2.9 copy-start.15
  577.1 1.8 copy-start.12
  580.6 1.7 copy-start.11
  585.9 160.5 %reduce-scatter.4.cloned.1.call-start = ((), (), s32[]{:S(2)}) async-start(), calls=%async_computation.8 | async-start | bytes 487424 | tf_op jit(solution)/shard_map/reduce_scatter | solution.py:139
  685.6 126.3 %reduce-scatter.6.cloned.1.call-start = ((), (), s32[]{:S(2)}) async-start(), calls=%async_computation.9 | async-start | bytes 487424 | tf_op jit(solution)/shard_map/reduce_scatter | solution.py:139
  685.7 3.8 copy-start.18
  685.7 3.8 copy-start.19
  689.4 188.5 %reduce-scatter.8.cloned.1.call-start = ((), (), s32[]{:S(2)}) async-start(), calls=%async_computation.10 | async-start | bytes 487424 | tf_op jit(solution)/shard_map/reduce_scatter | solution.py:139
Sparse Core Ops, SparseCore 0:
  401.9 154.3 all-reduce.5
  586.0 95.9 all-reduce.7
  686.2 60.2 reduce-scatter.3
  750.0 61.9 reduce-scatter.5
  816.0 61.9 reduce-scatter.7
where the time goes:
time: 889 us; the launch traced here: 886 us
  waiting for transfers between devices  622 us (70%)
  blocking collectives  100 us (11%)
  starting transfers between devices  41.1 us (5%)
  matrix products  40.5 us (5%)
  local copies, waits for them, and re-layouts  35.4 us (4%)
  other arithmetic  24.2 us (3%)
  between operations  23 us (3%)
    reduce_scatter x3, waiting for transfers between devices, local(): lax.psum_scatter(jnp.dot(hidden, w_down, preferred_element_type=jnp.float...  183 us
    psum x1, waiting for transfers between devices, local(): lax.psum(partial_value.astype(jnp.bfloat16), 'local').astype(jnp.float32)  154 us
    all_to_all x1, waiting for transfers between devices, local(): lax.all_to_all(onward, 'local', split_axis=0, concat_axis=0, tiled=True)  130 us
    psum x1, waiting for transfers between devices, local(): lax.psum(up_part.astype(jnp.bfloat16), 'node').astype(jnp.float32)  96.1 us
    all_gather x3, blocking collectives, local(): lax.all_gather(values, 'node', axis=0, tiled=True)  85.5 us
    all_to_all x1, waiting for transfers between devices, local(): lax.all_to_all(outbound, 'node', split_axis=0, concat_axis=0, tiled=True)  53.8 us
    all_to_all x3, starting transfers between devices, local(): lax.all_to_all(contexts[step_index], 'local', split_axis=1, concat_axis=0...  26.2 us
  transfers between devices with their start and end apart: 10, of which 8 were waited for; matrix products, arithmetic and copies ran while one was open for 5% of the time, Pallas kernels for 0%

commit v1 on v0

v1 whole, which is shorter than its diff:
```python
import functools

import jax
import jax.numpy as jnp
from jax import lax
from jax.experimental import pallas as pl
from jax.experimental.pallas import tpu as pltpu
from jax.sharding import PartitionSpec as P

MESH = pl.DeviceIdType.MESH
BF16, F32 = jnp.bfloat16, jnp.float32
D = 7168
QK_NOPE = 128
LATENT = 512
ROPE = 64
WIDTH = LATENT + ROPE
STEPS = 3
HEADS = 128
NODES, LOCALS = 8, 16
DEVS = NODES * LOCALS
CHIPS = LOCALS // 2
TILES = 128
EPS = 1e-06
SCALE = (QK_NOPE + ROPE) ** (-0.5)
NODE_ROWS = 96
SHARE = 48
COLS = 896
HID = 1152
NT = (((1,), (1,)), ((), ()))


def dot(a, b):
    return jnp.dot(a, b, preferred_element_type=F32)


def dot_nt(a, b):
    return lax.dot_general(a, b, NT, preferred_element_type=F32)


def rcopy(src, dst, send, recv, device):
    return pltpu.make_async_remote_copy(
        src_ref=src, dst_ref=dst, send_sem=send, recv_sem=recv, device_id=device, device_id_type=MESH
    )


def attend(query, fresh, key0, key1, length):
    s0 = dot(query, key0) * SCALE
    s1 = dot(query, key1) * SCALE
    sf = dot_nt(query, fresh) * SCALE
    rows, block = s0.shape
    column = lax.broadcasted_iota(jnp.int32, (rows, block), 1)
    s0 = jnp.where(column < length, s0, -jnp.inf)
    s1 = jnp.where(column + block < length, s1, -jnp.inf)
    step = lax.broadcasted_iota(jnp.int32, sf.shape, 0) // HEADS
    entry = lax.broadcasted_iota(jnp.int32, sf.shape, 1)
    sf = jnp.where(entry <= step, sf, -jnp.inf)
    top = jnp.maximum(
        jnp.max(jnp.maximum(s0, s1), axis=1, keepdims=True), jnp.max(sf, axis=1, keepdims=True)
    )
    w0 = jnp.exp(s0 - top)
    w1 = jnp.exp(s1 - top)
    wf = jnp.exp(sf - top)
    total = jnp.sum(w0 + w1, axis=1, keepdims=True) + jnp.sum(wf, axis=1, keepdims=True)
    context = dot_nt(w0.astype(BF16), key0[:LATENT])
    context += dot_nt(w1.astype(BF16), key1[:LATENT])
    context += dot(wf.astype(BF16), fresh[:, :LATENT])
    return context / total


def kernel(
    ints, tiles, query_stay, fresh_stay, pool, source, resid, gain,
    wuv_hbm, wout_hbm, wg_hbm, wu_hbm, wd_hbm,
    out,
    wuv, wout, wg, wu, wd,
    r1, s2, r2, query_arr, fresh_arr, ctx, ctx_send, ctx_recv, ctx_wide,
    values, proj, part, pair, share_send, share_recv, mixed,
    gu_send, gu_recv, sq_send, sq_recv, hidden,
    part2, pair2, share_send2, share_recv2,
    wsem, ready, sem, node_sem, local_sem, hid_sem, pair_sem, pair_sem2,
):
    n, l = lax.axis_index("node"), lax.axis_index("local")
    me = n * LOCALS + l
    core, chip = lax.rem(l, 2), l // 2
    sibling = (n, l + 1 - 2 * core)

    weights = [
        pltpu.make_async_copy(a, b, wsem.at[i])
        for i, (a, b) in enumerate(
            ((wuv_hbm, wuv), (wout_hbm, wout), (wg_hbm, wg), (wu_hbm, wu), (wd_hbm, wd))
        )
    ]
    for copy in weights:
        copy.start()

    barrier = pltpu.get_barrier_semaphore()

    def greet_node(i, c):
        pl.semaphore_signal(barrier, inc=1, device_id=(lax.rem(n + i, NODES), l), device_id_type=MESH)
        return c

    def greet_local(i, c):
        pl.semaphore_signal(barrier, inc=1, device_id=(n, lax.rem(l + i, LOCALS)), device_id_type=MESH)
        return c

    def greet_all(i, c):
        pl.semaphore_signal(ready, inc=1, device_id=(n, lax.rem(l + i, LOCALS)), device_id_type=MESH)
        return c

    lax.fori_loop(1, NODES, greet_node, 0)
    lax.fori_loop(1, LOCALS, greet_local, 0)
    pl.semaphore_wait(barrier, NODES - 1 + LOCALS - 1)
    lax.fori_loop(1, LOCALS, greet_all, 0)
    pl.semaphore_wait(ready, LOCALS - 1)

    def spread(i, c):
        p = lax.rem(me + i, DEVS)
        rcopy(tiles.at[p], r1.at[me], sem.at[0], sem.at[1], (p // LOCALS, lax.rem(p, LOCALS))).start()
        return c

    lax.fori_loop(1, DEVS, spread, 0)
    r1[me] = tiles[me]
    ctx[0] = attend(query_stay[...], fresh_stay[...], pool[ints[0]], pool[ints[1]], ints[4])
    both = pl.ds(0, DEVS - 1)
    rcopy(tiles.at[both], r1.at[both], sem.at[0], sem.at[1], (n, l)).wait()

    def sort(o, c):
        s2[o] = r1[ints[6 + o]]
        return c

    lax.fori_loop(0, DEVS, sort, 0)

    def deliver(i, c):
        p = lax.rem(me + i, DEVS)
        rcopy(s2.at[p], r2.at[me], sem.at[2], sem.at[3], (p // LOCALS, lax.rem(p, LOCALS))).start()
        return c

    lax.fori_loop(1, DEVS, deliver, 0)
    r2[me] = s2[me]
    rcopy(s2.at[both], r2.at[both], sem.at[2], sem.at[3], (n, l)).wait()
    for s in range(STEPS):
        for hb in range(HEADS // 16):
            for cb in range(5):
                query_arr[s * HEADS + hb * 16 : s * HEADS + hb * 16 + 16, cb * 128 : cb * 128 + 128] = r2[
                    (s * (HEADS // 16) + hb) * 5 + cb
                ]
    for cb in range(5):
        fresh_arr[:, cb * 128 : cb * 128 + 128] = r2[STEPS * (HEADS // 16) * 5 + cb]
    ctx[1] = attend(query_arr[:, :WIDTH], fresh_arr[:, :WIDTH], pool[ints[2]], pool[ints[3]], ints[5])

    def group(g):
        at = pl.multiple_of(g * 8, 8)
        pieces = [ctx[j, pl.ds(s * HEADS + at, 8), :] for j in range(2) for s in range(STEPS)]
        return jnp.concatenate(pieces, axis=0).astype(BF16)

    def send_group(i, c):
        g = lax.rem(l + i, LOCALS)
        ctx_send[g] = group(g)
        rcopy(ctx_send.at[g], ctx_recv.at[l], sem.at[4], sem.at[5], (n, g)).start()
        return c

    lax.fori_loop(1, LOCALS, send_group, 0)
    ctx_recv[l] = group(l)
    weights[0].wait()
    others = pl.ds(0, LOCALS - 1)
    rcopy(ctx_send.at[others], ctx_recv.at[others], sem.at[4], sem.at[5], (n, l)).wait()
    for t in range(LATENT // 128):
        ctx_wide[t] = ctx_recv[:, :, t * 128 : t * 128 + 128].reshape(LOCALS * SHARE, 128).astype(F32)
    for h in range(8):
        rows = [ctx_wide[t, pl.ds(h, NODE_ROWS, stride=8), :] for t in range(LATENT // 128)]
        rows = jnp.concatenate(rows, axis=1).astype(BF16)
        values[n, :, h * 128 : h * 128 + 128] = dot(rows, wuv[h]).astype(BF16)

    def send_values(i, c):
        p = lax.rem(n + i, NODES)
        rcopy(values.at[n], values.at[n], sem.at[6], node_sem.at[n], (p, l)).start()
        return c

    lax.fori_loop(1, NODES, send_values, 0)
    weights[1].wait()
    proj[n] = dot(values[n], wout[...]).astype(BF16)

    def project(i, c):
        p = lax.rem(n + NODES - i, NODES)
        rcopy(values.at[p], values.at[p], sem.at[6], node_sem.at[p], (n, l)).wait_recv()
        proj[p] = dot(values[p], wout[...]).astype(BF16)
        return c

    lax.fori_loop(1, NODES, project, 0)
    sent = pl.ds(0, NODES - 1)
    rcopy(values.at[sent], values.at[sent], sem.at[6], node_sem.at[0], (n, l)).wait_send()

    def scatter(make, part, pair, pair_sem, share_send, share_recv, send, recv):
        def produce(i, c):
            q = lax.rem(chip // 2 + i, 4)
            block = make(q).astype(BF16).reshape(4, SHARE, COLS)
            for k in range(4):
                part[k % 2, 2 * q + k // 2] = block[k]
            two = pl.ds(2 * q, 2)
            rcopy(part.at[1 - core, two], pair.at[two], send.at[0], pair_sem.at[q], sibling).start()
            return c

        lax.fori_loop(1, 5, produce, 0)

        def combine(i, c):
            q = lax.rem(chip // 2 + i, 4)
            two = pl.ds(2 * q, 2)
            rcopy(part.at[1 - core, two], pair.at[two], send.at[0], pair_sem.at[q], sibling).wait_recv()
            for k in range(2):
                to = 2 * q + k
                total = (part[core, to].astype(F32) + pair[to].astype(F32)).astype(BF16)

                @pl.when(to != chip)
                def _():
                    share_send[to] = total
                    rcopy(
                        share_send.at[to], share_recv.at[chip], send.at[1], recv, (n, to * 2 + core)
                    ).start()

                @pl.when(to == chip)
                def _():
                    share_recv[chip] = total

            return c

        lax.fori_loop(1, 5, combine, 0)
        rcopy(part.at[0], pair, send.at[0], pair_sem.at[0], sibling).wait_send()
        seven = pl.ds(0, CHIPS - 1)
        rcopy(share_send.at[seven], share_recv.at[seven], send.at[1], recv, sibling).wait()
        return jnp.sum(share_recv[...].astype(F32), axis=0)

    def permuted(q):
        rows = source[pl.ds(pl.multiple_of(q * 192, 192), 192), :]
        column = lax.broadcasted_iota(jnp.int32, (192, 768), 1)
        pick = jnp.where(rows == column, 1.0, 0.0).astype(BF16)
        return dot(pick, proj[...].reshape(768, COLS))

    attn = scatter(
        permuted, part, pair, pair_sem, share_send, share_recv, sem.at[pl.ds(8, 2)], sem.at[10]
    )
    mine = (resid[...].astype(F32) + attn).astype(BF16)
    mixed[l] = mine

    def send_mixed(i, c):
        to = lax.rem(chip + i, CHIPS)
        rcopy(mixed.at[l], mixed.at[l], sem.at[11], local_sem.at[l], (n, to * 2 + core)).start()
        return c

    lax.fori_loop(1, CHIPS, send_mixed, 0)
    rcopy(mixed.at[l], mixed.at[l], sem.at[12], local_sem.at[l], sibling).start()

    def pass_mixed(i, c):
        b = lax.rem(chip + CHIPS - i, CHIPS) * 2 + core
        rcopy(mixed.at[b], mixed.at[b], sem.at[11], local_sem.at[b], (n, l)).wait_recv()
        rcopy(mixed.at[b], mixed.at[b], sem.at[12], local_sem.at[b], sibling).start()
        return c

    lax.fori_loop(1, CHIPS, pass_mixed, 0)

    def take_mixed(i, c):
        b = lax.rem(chip + CHIPS - i, CHIPS) * 2 + 1 - core
        rcopy(mixed.at[b], mixed.at[b], sem.at[11], local_sem.at[b], (n, l)).wait_recv()
        return c

    lax.fori_loop(0, CHIPS, take_mixed, 0)
    seven = pl.ds(0, CHIPS - 1)
    rcopy(mixed.at[seven], mixed.at[seven], sem.at[11], local_sem.at[0], (n, l)).wait_send()
    eight = pl.ds(0, CHIPS)
    rcopy(mixed.at[eight], mixed.at[eight], sem.at[12], local_sem.at[0], (n, l)).wait_send()

    weights[2].wait()
    weights[3].wait()

    def expand(i, c):
        q = lax.rem(n // 2 + i, 4)
        wide = mixed[pl.ds(4 * q, 4)].reshape(192, COLS).astype(F32)
        scaled = (wide * gain[...]).astype(BF16)
        square = wide * wide
        lanes = square[:, :128]
        for t in range(1, COLS // 128):
            lanes += square[:, t * 128 : t * 128 + 128]
        gate = dot(scaled, wg[...]).astype(BF16)
        up = dot(scaled, wu[...]).astype(BF16)
        for k in range(2):
            to = 2 * q + k
            gu_send[to, :, :HID] = gate[k * NODE_ROWS : (k + 1) * NODE_ROWS]
            gu_send[to, :, HID:] = up[k * NODE_ROWS : (k + 1) * NODE_ROWS]
            sq_send[to] = jnp.zeros((8, 128), F32)
            sq_send[to, :, :NODE_ROWS] = lax.dot_general(
                jnp.ones((8, 128), F32),
                lanes[k * NODE_ROWS : (k + 1) * NODE_ROWS],
                NT,
                precision=lax.Precision.HIGHEST,
                preferred_element_type=F32,
            )

            @pl.when(to != n)
            def _():
                rcopy(gu_send.at[to], gu_recv.at[n], sem.at[13], sem.at[14], (to, l)).start()
                rcopy(sq_send.at[to], sq_recv.at[n], sem.at[15], sem.at[16], (to, l)).start()

        return c

    lax.fori_loop(1, 5, expand, 0)
    gu_recv[n] = gu_send[n]
    sq_recv[n] = sq_send[n]
    rcopy(sq_send.at[sent], sq_recv.at[sent], sem.at[15], sem.at[16], (n, l)).wait()
    mean = jnp.sum(sq_recv[...], axis=0) / D + EPS
    inverse = jnp.broadcast_to(lax.rsqrt(mean)[:1], (NODE_ROWS, 128))
    diagonal = lax.broadcasted_iota(jnp.int32, (NODE_ROWS, 128), 0) == lax.broadcasted_iota(
        jnp.int32, (NODE_ROWS, 128), 1
    )
    inverse = jnp.sum(jnp.where(diagonal, inverse, 0.0), axis=1, keepdims=True)
    rcopy(gu_send.at[sent], gu_recv.at[sent], sem.at[13], sem.at[14], (n, l)).wait()

    def activate(t, c):
        at = pl.multiple_of(t * 128, 128)
        gate = gu_recv[0, :, pl.ds(at, 128)].astype(F32)
        up = gu_recv[0, :, pl.ds(at + HID, 128)].astype(F32)
        for k in range(1, NODES):
            gate += gu_recv[k, :, pl.ds(at, 128)].astype(F32)
            up += gu_recv[k, :, pl.ds(at + HID, 128)].astype(F32)
        gate *= inverse
        up *= inverse
        hidden[n, :, pl.ds(at, 128)] = (gate / (1.0 + jnp.exp(-gate)) * up).astype(BF16)
        return c

    lax.fori_loop(0, HID // 128, activate, 0)

    def send_hidden(i, c):
        p = lax.rem(n + i, NODES)
        rcopy(hidden.at[n], hidden.at[n], sem.at[17], hid_sem.at[n], (p, l)).start()
        return c

    lax.fori_loop(1, NODES, send_hidden, 0)
    weights[4].wait()

    def take_hidden(i, c):
        p = lax.rem(n + NODES - i, NODES)
        rcopy(hidden.at[p], hidden.at[p], sem.at[17], hid_sem.at[p], (n, l)).wait_recv()
        return c

    lax.fori_loop(1, NODES, take_hidden, 0)
    rcopy(hidden.at[sent], hidden.at[sent], sem.at[17], hid_sem.at[0], (n, l)).wait_send()

    def down(q):
        return dot(hidden[pl.ds(2 * q, 2)].reshape(192, HID), wd[...])

    block_out = scatter(
        down, part2, pair2, pair_sem2, share_send2, share_recv2, sem.at[pl.ds(18, 2)], sem.at[20]
    )
    out[...] = (mixed[l].astype(F32) + block_out).astype(BF16)


def local(
    cache_pool, block_table, lengths, mig_slot, mig_dest, queries, new_entries, residual,
    w_uv, w_out, norm_gain, w_gate, w_up, w_down,
):
    n, l = lax.axis_index("node"), lax.axis_index("local")
    me = n * LOCALS + l
    leave = mig_slot[me]
    stay = 1 - leave
    own = lax.dynamic_slice_in_dim(lengths, me * 2, 2)
    ints = jnp.concatenate(
        [block_table[stay], block_table[leave], own[stay][None], own[leave][None], mig_dest]
    )
    by_slot = queries.reshape(STEPS, 2, HEADS, WIDTH)
    query_stay = lax.dynamic_index_in_dim(by_slot, stay, 1, keepdims=False).reshape(-1, WIDTH)
    leaving = lax.dynamic_index_in_dim(by_slot, leave, 1, keepdims=False)
    leaving = jnp.pad(leaving, ((0, 0), (0, 0), (0, 640 - WIDTH)))
    leaving = leaving.reshape(STEPS, HEADS // 16, 16, 5, 128).transpose(0, 1, 3, 2, 4).reshape(-1, 16, 128)
    fresh_stay = jnp.pad(lax.dynamic_index_in_dim(new_entries, stay, 1, keepdims=False), ((0, 13), (0, 0)))
    fresh_leave = lax.dynamic_index_in_dim(new_entries, leave, 1, keepdims=False)
    fresh_leave = jnp.pad(fresh_leave, ((0, 13), (0, 640 - WIDTH)))
    fresh_leave = fresh_leave.reshape(16, 5, 128).transpose(1, 0, 2)
    tiles = jnp.concatenate([leaving, fresh_leave, jnp.zeros((3, 16, 128), BF16)])
    device = jnp.arange(DEVS, dtype=jnp.int32)
    anchor = jnp.argmax(mig_dest[None, :] == device[:, None], axis=1).astype(jnp.int32)
    slot = jnp.arange(2, dtype=jnp.int32)
    request = jnp.where(slot[None, :] == mig_slot[:, None], anchor[:, None] * 2 + 1, device[:, None] * 2)
    source = request[:, :, None] * STEPS + jnp.arange(STEPS, dtype=jnp.int32)
    source = source.reshape(DEVS * 2 * STEPS, 1)
    resid = lax.dynamic_slice_in_dim(residual, l * 16, 16, 1).transpose(1, 0, 2).reshape(SHARE, COLS)

    vm = pl.BlockSpec(memory_space=pltpu.VMEM)
    hbm = pl.BlockSpec(memory_space=pl.ANY)
    dma = pltpu.SemaphoreType.DMA
    V = pltpu.VMEM
    result = pl.pallas_call(
        kernel,
        out_shape=jax.ShapeDtypeStruct((SHARE, COLS), BF16),
        in_specs=[pl.BlockSpec(memory_space=pltpu.SMEM)] + [vm] * 7 + [hbm] * 5,
        out_specs=vm,
        scratch_shapes=[
            V((8, LATENT, 128), BF16), V((1024, COLS), BF16), V((COLS, HID), BF16), V((COLS, HID), BF16),
            V((HID, COLS), BF16),
            V((DEVS, 16, 128), BF16), V((DEVS, 16, 128), BF16), V((DEVS, 16, 128), BF16),
            V((STEPS * HEADS, 640), BF16), V((16, 640), BF16),
            V((2, STEPS * HEADS, LATENT), F32),
            V((LOCALS, SHARE, LATENT), BF16), V((LOCALS, SHARE, LATENT), BF16),
            V((LATENT // 128, LOCALS * SHARE, 128), F32),
            V((NODES, NODE_ROWS, 1024), BF16), V((NODES, NODE_ROWS, COLS), BF16),
            V((2, CHIPS, SHARE, COLS), BF16), V((CHIPS, SHARE, COLS), BF16),
            V((CHIPS, SHARE, COLS), BF16), V((CHIPS, SHARE, COLS), BF16),
            V((LOCALS, SHARE, COLS), BF16),
            V((NODES, NODE_ROWS, 2 * HID), BF16), V((NODES, NODE_ROWS, 2 * HID), BF16),
            V((NODES, 8, 128), F32), V((NODES, 8, 128), F32),
            V((NODES, NODE_ROWS, HID), BF16),
            V((2, CHIPS, SHARE, COLS), BF16), V((CHIPS, SHARE, COLS), BF16),
            V((CHIPS, SHARE, COLS), BF16), V((CHIPS, SHARE, COLS), BF16),
            dma((5,)), pltpu.SemaphoreType.REGULAR, dma((21,)), dma((NODES,)), dma((LOCALS,)),
            dma((NODES,)), dma((4,)), dma((4,)),
        ],
        compiler_params=pltpu.CompilerParams(
            collective_id=0, has_side_effects=True, vmem_limit_bytes=60 * 2**20
        ),
        name="layer",
    )(
        ints, tiles, query_stay, fresh_stay, cache_pool, source, resid, norm_gain.reshape(1, COLS),
        w_uv, w_out, w_gate, w_up, w_down,
    )
    return result.reshape(16, STEPS, COLS).transpose(1, 0, 2)


def solution(mesh):
    in_specs = (
        P(("node", "local"), None, None),
        P(("node", "local"), None),
        P(),
        P(),
        P(),
        P(None, ("node", "local"), None),
        P(None, ("node", "local"), None),
        P(None, None, "node"),
        P("local", None, None),
        P("local", "node"),
        P("node"),
        P("node", "local"),
        P("node", "local"),
        P("local", "node"),
    )
    out_specs = P(None, "local", "node")
    return jax.shard_map(local, mesh=mesh, in_specs=in_specs, out_specs=out_specs, check_vma=False)
```

time: 889 us -> 201 us (0.23)
  waiting for transfers between devices: 622 us -> 0 us
  Pallas kernels: 0 us -> 183 us
  blocking collectives: 100 us -> 0 us
  starting transfers between devices: 41.1 us -> 0 us
  matrix products: 40.5 us -> 0 us
  local copies, waits for them, and re-layouts: 35.4 us -> 12.8 us
  other arithmetic: 24.2 us -> 2.01 us
  between operations: 23 us -> 3.4 us
    psum x2 -> x0, waiting for transfers between devices: 251 us -> none  [the longest x1 154 us: local(): lax.psum(partial_value.astype(jnp.bfloat16), 'local').astype(jnp.float32)]
    all_to_all x5 -> x0, waiting for transfers between devices: 187 us -> none  [the longest x1 130 us: local(): lax.all_to_all(onward, 'local', split_axis=0, concat_axis=0, tiled=True)]
    reduce_scatter x3 -> x0, waiting for transfers between devices: 183 us -> none  [local(): lax.psum_scatter(jnp.dot(hidden, w_down, preferred_element_type=jnp.float...]
    pallas_call x0 -> x1, Pallas kernels: none -> 183 us  [local(): pl.pallas_call(kernel, out_shape=jax.ShapeDtypeStruct((SHARE, COLS), BF16...]
    all_gather x3 -> x0, blocking collectives: 85.5 us -> none  [local(): lax.all_gather(values, 'node', axis=0, tiled=True)]
    all_to_all x5 -> x0, starting transfers between devices: 40.9 us -> none  [the longest x3 26.2 us: local(): lax.all_to_all(contexts[step_index], 'local', split_axis=1, concat_axis=0...]
    dot_general x26 -> x0, matrix products: 40.5 us -> none  [the longest x3 10.5 us: local(): jnp.dot(hidden, w_down, preferred_element_type=jnp.float32)]
    psum x1 -> x0, blocking collectives: 14.9 us -> none  [local(): squares = lax.psum(jnp.sum(mixed_wide * mixed_wide, axis=1), 'node')]
  transfers between devices with their start and end apart: 10 -> 0, of which waited for: 8 -> 0; matrix products, arithmetic and copies ran while one was open for 5% -> 0% of each run, Pallas kernels for 0% -> 0%
where the time goes in v1:
time: 201 us
  Pallas kernels  183 us (91%)
  local copies, waits for them, and re-layouts  12.8 us (6%)
  between operations  3.4 us (2%)
    pallas_call x1, Pallas kernels, local(): pl.pallas_call(kernel, out_shape=jax.ShapeDtypeStruct((SHARE, COLS), BF16...  183 us

profile of v1, /device:TPU:1, one launch (start us, length us, event | category | flops | bytes accessed | tf_op | source)
XLA Modules:
  0.0 200.8 jit_solution(11810879661157716942)
XLA Ops:
  0.0 0.0 copy-start
  0.0 1.3 dynamic_slice.37
  4.6 2.6 %reshape.109 = bf16[3,2,128,576]{3,2,1,0:T(8,128)(2,1)S(1)} reshape(bf16[3,2,73728]{2,1,0:T(2,128)(2,1)} %param.19) | data formatting | bytes 1769472 | tf_op jit(solution)/shard_map/reshape | solution.py:366
  7.2 0.9 constant_dynamic-slice_fusion.1
  8.1 0.0 copy-start.1
  8.1 0.0 copy-start.3
  8.1 0.0 copy-start.4
  8.1 0.0 copy-start.6
  8.1 0.6 reshape.110
  8.7 0.0 copy-start.5
  8.7 0.0 copy-start.2
  8.7 0.1 copy.23
  8.8 0.0 copy-done.1
  8.9 0.1 pad.17.clone
  9.0 1.0 maximum_maximum_fusion.tiles
  10.0 0.6 pad.14.fresh_stay
  10.6 0.0 copy-done.3
  10.6 0.7 fusion.2
  11.2 0.0 copy-done.4
  11.3 0.0 copy-done.6
  11.3 1.9 concatenate.6.ints
  13.2 0.0 copy-done
  13.3 0.7 reshape.114.resid
  14.0 0.7 iota_reduce_fusion
  14.7 0.0 copy-done.5
  14.7 0.1 select_multiply_fusion
  14.8 0.2 iota_add_fusion
  15.0 1.0 add.77.source
  16.0 0.0 copy-done.2
  16.0 0.6 reshape.115.gain
  16.6 182.6 %layer.1 = bf16[48,896]{1,0:T(8,128)(2,1)} custom-call(s32[134]{0:T(256)} %concatenate.6.ints, bf16[128,16,128]{2,1,0:T(8,128)(2,1)} %maximum_maximum_fusion.tiles, bf16[384,576]{1,0:T(8,128)(2,1)} %bitcast.26, bf16[16,576]{1,0:T(8,128)(2,1)} %pad.14.fresh_stay, bf16[4,576,256]{2,1,0:T(8,128)(2,1)} %pool.1, s32[768,1]{1,0:T(8,128)} %add.77.source, ...), custom_call_target="tpu_custom_call" | custom-call | tf_op jit(solution)/shard_map/layer/pallas_call | solution.py:388
  199.3 0.9 reshape.116
  200.2 0.6 copy.27
  (9 shorter events, 0.2 us)
Async XLA Ops:
  0.0 13.2 %copy-start = (bf16[3,256,896]{2,1,0:T(8,128)(2,1)S(1)}, bf16[3,256,896]{2,1,0:T(8,128)(2,1)}, u32[]{:S(2)}) copy-start(bf16[3,256,896]{2,1,0:T(8,128)(2,1)} %param.21) | copy-start | bytes 4128772
  8.1 0.8 copy-start.1
  8.1 2.5 %copy-start.3 = (s32[256]{0:T(256)S(1)}, s32[256]{0:T(256)}, u32[]{:S(2)}) copy-start(s32[256]{0:T(256)} %param.16) | copy-start | bytes 3076
  8.1 3.1 %copy-start.4 = (s32[2,2]{1,0:T(2,128)S(1)}, s32[2,2]{1,0:T(2,128)}, u32[]{:S(2)}) copy-start(s32[2,2]{1,0:T(2,128)} %param.15) | copy-start | bytes 52
  8.1 3.1 %copy-start.6 = (s32[128]{0:T(128)S(1)}, s32[128]{0:T(128)}, u32[]{:S(2)}) copy-start(s32[128]{0:T(128)} %param.18) | copy-start | bytes 1540
  8.7 6.0 %copy-start.5 = (s32[128]{0:T(128)S(1)}, s32[128]{0:T(128)}, u32[]{:S(2)}) copy-start(s32[128]{0:T(128)} %param.17) | copy-start | bytes 1540
  8.7 7.3 %copy-start.2 = (f32[896]{0:T(1024)S(1)}, f32[896]{0:T(1024)}, u32[]{:S(2)}) copy-start(f32[896]{0:T(1024)} %param.24) | copy-start | bytes 10756

commit v2 on v0

v2 whole, which is shorter than its diff:
```python
import jax
import jax.numpy as jnp
from jax import lax
from jax.experimental import pallas as pl
from jax.experimental.pallas import tpu as pltpu
from jax.sharding import PartitionSpec as P

MESH = pl.DeviceIdType.MESH
BF16, F32 = jnp.bfloat16, jnp.float32
D = 7168
QK_NOPE = 128
LATENT = 512
ROPE = 64
WIDTH = LATENT + ROPE
STEPS = 3
HEADS = 128
NODES, LOCALS = 8, 16
DEVS = NODES * LOCALS
EPS = 1e-06
SCALE = (QK_NOPE + ROPE) ** (-0.5)
ROWS = 48
BATCH = NODES * ROWS
COLS = 896
HALF = 512
OFFSET = COLS - HALF
HID = 1152
KEYS = 640
NT = (((1,), (1,)), ((), ()))


def dot(a, b):
    return jnp.dot(a, b, preferred_element_type=F32)


def dot_nt(a, b):
    return lax.dot_general(a, b, NT, preferred_element_type=F32)


def iota(shape, dim):
    return lax.broadcasted_iota(jnp.int32, shape, dim)


def rcopy(src, dst, send, recv, device):
    return pltpu.make_async_remote_copy(
        src_ref=src, dst_ref=dst, send_sem=send, recv_sem=recv, device_id=device, device_id_type=MESH
    )


def attend(query, fresh, key0, key1, length):
    s0 = dot(query, key0) * SCALE
    s1 = dot(query, key1) * SCALE
    sf = dot_nt(query, fresh) * SCALE
    rows, block = s0.shape
    column = iota((rows, block), 1)
    s0 = jnp.where(column < length, s0, -jnp.inf)
    s1 = jnp.where(column + block < length, s1, -jnp.inf)
    step = iota(sf.shape, 0) // HEADS
    sf = jnp.where(iota(sf.shape, 1) <= step, sf, -jnp.inf)
    top = jnp.maximum(
        jnp.max(jnp.maximum(s0, s1), axis=1, keepdims=True), jnp.max(sf, axis=1, keepdims=True)
    )
    w0 = jnp.exp(s0 - top)
    w1 = jnp.exp(s1 - top)
    wf = jnp.exp(sf - top)
    total = jnp.sum(w0 + w1, axis=1, keepdims=True) + jnp.sum(wf, axis=1, keepdims=True)
    context = dot_nt(w0.astype(BF16), key0[:LATENT])
    context += dot_nt(w1.astype(BF16), key1[:LATENT])
    context += dot(wf.astype(BF16), fresh[:, :LATENT])
    return context / total


class Group:
    def __init__(self, pair, ring, block, device):
        self.p, self.r = pair, ring
        self.q = 1 - pair
        self.up, self.dn, self.op = lax.rem(ring + 1, 4), lax.rem(ring + 3, 4), lax.rem(ring + 2, 4)
        self.block, self.device = block, device


class Sems:
    def __init__(self, ref):
        self.ref, self.used, self.sent = ref, 0, []

    def take(self, count):
        first = self.used
        self.used += count
        return [self.ref.at[first + i] for i in range(count)]

    def start(self, src, dst, recv, device):
        copy = rcopy(src, dst, self.take(1)[0], recv, device)
        copy.start()
        self.sent.append(copy)


def arrived(ref, recv, here):
    rcopy(ref, ref, recv, recv, here).wait_recv()


def gather8(buf, g, sems, here, seen=None):
    width = buf.shape[-1] // 256 * 128
    lo, hi = pl.ds(0, width), pl.ds(width, buf.shape[-1] - width)
    recv = sems.take(8)
    b = g.block
    seen = seen or (lambda block: None)

    def send(block, to, index, cols=None):
        ref = buf.at[block] if cols is None else buf.at[block, :, cols]
        sems.start(ref, ref, recv[index], g.device(*to))

    def take(block, index, cols=None):
        arrived(buf.at[block] if cols is None else buf.at[block, :, cols], recv[index], here)

    own = b(g.p, g.r)
    send(own, (g.p, g.up), 2)
    send(own, (g.p, g.dn), 1)
    send(own, (g.q, g.r), 0)
    seen(own)
    yield
    take(b(g.p, g.up), 1)
    send(b(g.p, g.up), (g.p, g.dn), 5, lo)
    seen(b(g.p, g.up))
    take(b(g.p, g.dn), 2)
    send(b(g.p, g.dn), (g.p, g.up), 6, hi)
    seen(b(g.p, g.dn))
    take(b(g.q, g.r), 0)
    send(b(g.q, g.r), (g.p, g.up), 4)
    send(b(g.q, g.r), (g.p, g.dn), 3)
    seen(b(g.q, g.r))
    yield
    take(b(g.p, g.op), 5, lo)
    take(b(g.p, g.op), 6, hi)
    send(b(g.p, g.op), (g.q, g.r), 7)
    seen(b(g.p, g.op))
    yield
    take(b(g.q, g.up), 3)
    seen(b(g.q, g.up))
    take(b(g.q, g.dn), 4)
    seen(b(g.q, g.dn))
    take(b(g.q, g.op), 7)
    seen(b(g.q, g.op))


def scatter8(part, g, sems, here, own_plane, ra, rb, rc, rd, re, sc, sd, se):
    width = part.shape[-1] // 2
    halves = (pl.ds(0, width), pl.ds(width, width))
    recv = sems.take(10)
    b = g.block

    def wide(ref, *at):
        return ref[at].astype(F32)

    sems.start(part.at[b(g.q, g.op)], ra, recv[0], g.device(g.q, g.r))
    sems.start(part.at[b(g.q, g.up)], rb.at[0], recv[1], g.device(g.p, g.up))
    sems.start(part.at[b(g.q, g.dn)], rb.at[1], recv[2], g.device(g.p, g.dn))
    own_plane()
    up, dn = b(g.p, g.up), b(g.p, g.dn)
    sems.start(part.at[up, :, halves[1]], re.at[0, :, halves[1]], recv[6], g.device(g.p, g.up))
    sems.start(part.at[dn, :, halves[0]], re.at[1, :, halves[0]], recv[7], g.device(g.p, g.dn))
    yield
    arrived(ra, recv[0], here)
    sc[...] = (wide(part, b(g.p, g.op)) + wide(ra, ...)).astype(BF16)
    sems.start(sc.at[:, halves[0]], rc.at[0], recv[3], g.device(g.p, g.up))
    sems.start(sc.at[:, halves[1]], rc.at[1], recv[4], g.device(g.p, g.dn))
    arrived(rb.at[0], recv[1], here)
    arrived(rb.at[1], recv[2], here)
    sd[...] = (wide(part, b(g.q, g.r)) + wide(rb, 0) + wide(rb, 1)).astype(BF16)
    sems.start(sd, rd, recv[5], g.device(g.q, g.r))
    yield
    arrived(rc.at[0], recv[3], here)
    se[0] = (wide(part, up, slice(None), halves[0]) + wide(rc, 0)).astype(BF16)
    sems.start(se.at[0], re.at[0, :, halves[0]], recv[8], g.device(g.p, g.up))
    arrived(rc.at[1], recv[4], here)
    se[1] = (wide(part, dn, slice(None), halves[1]) + wide(rc, 1)).astype(BF16)
    sems.start(se.at[1], re.at[1, :, halves[1]], recv[9], g.device(g.p, g.dn))
    yield
    arrived(rd, recv[5], here)
    arrived(re.at[0, :, halves[1]], recv[6], here)
    arrived(re.at[1, :, halves[0]], recv[7], here)
    arrived(re.at[0, :, halves[0]], recv[8], here)
    arrived(re.at[1, :, halves[1]], recv[9], here)


def scatter8_shapes(cols):
    V = pltpu.VMEM
    return [
        V((2, ROWS, cols), BF16), V((2, 2, ROWS, cols), BF16), V((2, 2, ROWS, cols // 2), BF16),
        V((2, ROWS, cols), BF16), V((2, 2, ROWS, cols), BF16), V((2, ROWS, cols), BF16),
        V((2, ROWS, cols), BF16), V((2, 2, ROWS, cols // 2), BF16),
    ]


def kernel(
    table, lengths, slot_s, dest_s, slot_v, dest_v, gain, fresh_all,
    query_hbm, pool_hbm, resid_hbm, wuv_hbm, wout_hbm, wg_hbm, wu_hbm, wd_hbm,
    out, *scratch,
):
    refs = list(scratch)
    take = lambda count=1: [refs.pop(0) for _ in range(count)]
    query, pool, resid, wuv, wout, wg, wu, wd = take(8)
    tiles, r1, s2, r2, query_arr, fresh = take(6)
    ctx, ctx_send, ctx_recv, wide = take(4)
    values, part, pair, summed, mixed = take(5)
    attn_bufs = take(8)
    gu, sq_send, sq_recv, hidden = take(4)
    gu_bufs = take(8)
    part2, pair2, summed2, last, done = take(5)
    down_bufs = take(8)
    wsem, ready, far, ref_a, ref_b = take(5)

    n, l = lax.axis_index("node"), lax.axis_index("local")
    me = n * LOCALS + l
    here = (n, l)
    core, chip = lax.rem(l, 2), l // 2
    sibling = (n, l + 1 - 2 * core)
    mine = pl.multiple_of(core * OFFSET, 128)
    theirs = pl.multiple_of((1 - core) * OFFSET, 128)
    node = Group(n // 4, lax.rem(n, 4), lambda p, r: p * 4 + r, lambda p, r: (p * 4 + r, l))
    chips = Group(
        lax.rem(chip, 2), chip // 2, lambda p, r: r * 2 + p, lambda p, r: (n, (r * 2 + p) * 2 + core)
    )

    barrier = pltpu.get_barrier_semaphore()

    def greet_node(i, c):
        pl.semaphore_signal(barrier, inc=1, device_id=(lax.rem(n + i, NODES), l), device_id_type=MESH)
        return c

    def greet_local(i, c):
        pl.semaphore_signal(barrier, inc=1, device_id=(n, lax.rem(l + i, LOCALS)), device_id_type=MESH)
        return c

    def greet_all(i, c):
        pl.semaphore_signal(ready, inc=1, device_id=(n, lax.rem(l + i, LOCALS)), device_id_type=MESH)
        return c

    lax.fori_loop(1, NODES, greet_node, 0)
    lax.fori_loop(1, LOCALS, greet_local, 0)

    loads = [
        pltpu.make_async_copy(a, b, wsem.at[i])
        for i, (a, b) in enumerate(
            (
                (query_hbm, query), (pool_hbm, pool), (wuv_hbm, wuv), (wout_hbm, wout),
                (resid_hbm.at[:, pl.ds(chip * 32, 32), :], resid),
                (wg_hbm, wg), (wu_hbm, wu), (wd_hbm, wd),
            )
        )
    ]
    for copy in loads:
        copy.start()

    leave = slot_s[me]
    stay = 1 - leave

    fresh[...] = jnp.zeros(fresh.shape, BF16)
    both_fresh = fresh_all[...].astype(F32)
    fresh[0, :STEPS, :WIDTH] = jnp.where(stay == 0, both_fresh[:, 0], both_fresh[:, 1]).astype(BF16)
    fresh[1, :STEPS, :WIDTH] = jnp.where(stay == 1, both_fresh[:, 0], both_fresh[:, 1]).astype(BF16)
    loads[0].wait()
    blocks = HEADS // 16
    for s in range(STEPS):
        for hb in range(blocks):
            for cb in range(5):
                width = min(128, WIDTH - cb * 128)
                tiles[(s * blocks + hb) * 5 + cb, :, :width] = query[
                    s * 2 + leave, hb * 16 : hb * 16 + 16, cb * 128 : cb * 128 + width
                ]
    for cb in range(5):
        tiles[STEPS * blocks * 5 + cb] = fresh[1, :, cb * 128 : cb * 128 + 128]

    pl.semaphore_wait(barrier, NODES - 1 + LOCALS - 1)
    lax.fori_loop(1, LOCALS, greet_all, 0)
    pl.semaphore_wait(ready, LOCALS - 1)

    def spread(i, c):
        p = lax.rem(me + i, DEVS)
        rcopy(tiles.at[p], r1.at[me], far.at[0], far.at[1], (p // LOCALS, lax.rem(p, LOCALS))).start()
        return c

    lax.fori_loop(1, DEVS, spread, 0)
    r1[me] = tiles[me]
    loads[1].wait()

    def attention(j):
        if j == 0:
            request, new = stay, fresh[0, :, :WIDTH]
            rows = jnp.concatenate([query[s * 2 + stay] for s in range(STEPS)], axis=0)
        else:
            request, new = leave, fresh[1, :, :WIDTH]
            rows = query_arr[:, :WIDTH]
        key0, key1 = pool[table[request, 0]], pool[table[request, 1]]
        ctx[j] = attend(rows, new, key0, key1, lengths[me * 2 + request])

    others = pl.ds(0, LOCALS - 1)

    def send_context(j, sems):
        def group(g):
            at = pl.multiple_of(g * 8, 8)
            rows = jnp.concatenate([ctx[j, pl.ds(s * HEADS + at, 8), :] for s in range(STEPS)], axis=0)
            return jnp.concatenate([rows[:, :256], rows[:, 256:]], axis=0).astype(BF16)

        send, recv = sems.take(2)

        def send_group(i, c):
            g = lax.rem(l + i, LOCALS)
            ctx_send[j, g] = group(g)
            rcopy(ctx_send.at[j, g], ctx_recv.at[j, l], send, recv, (n, g)).start()
            return c

        lax.fori_loop(1, LOCALS, send_group, 0)
        ctx_recv[j, l] = group(l)
        return rcopy(ctx_send.at[j, others], ctx_recv.at[j, others], send, recv, here)

    def select(rows, columns, test):
        return jnp.where(test(iota((rows, columns), 0), iota((rows, columns), 1)), 1.0, 0.0).astype(BF16)

    def slots(rows, device):
        lanes = jnp.broadcast_to(slot_v[...], (rows, DEVS)).astype(F32)
        at = device(iota((rows, DEVS), 0)) == iota((rows, DEVS), 1)
        return jnp.sum(jnp.where(at, lanes, 0.0), axis=1, keepdims=True).astype(jnp.int32)

    def halves(product, part, pair, summed, j, sems):
        part[j] = product.reshape(NODES, ROWS, COLS)
        recv = sems.take(1)[0]
        sems.start(part.at[j, :, :, pl.ds(theirs, HALF)], pair.at[j], recv, sibling)
        yield
        arrived(pair.at[j], recv, here)
        summed[j] = (part[j, :, :, pl.ds(mine, HALF)].astype(F32) + pair[j].astype(F32)).astype(BF16)

    def total(bufs, part, g, j):
        own = part[j, g.block(g.p, g.r)].astype(F32)
        rd, re = bufs[3], bufs[4]
        return own + rd[j].astype(F32) + re[j, 0].astype(F32) + re[j, 1].astype(F32)

    def chain(j, sems, context):
        if j == 0:
            loads[2].wait()
        context.wait()
        for t in range(2):
            got = ctx_recv[j, :, :, t * 128 : t * 128 + 128].astype(F32)
            for half in range(2):
                for s in range(STEPS):
                    at = half * 24 + s * 8
                    wide[half * 2 + t, s * 128 : s * 128 + 128] = got[:, at : at + 8].reshape(128, 128)
        for h in range(8):
            rows = [wide[t, pl.ds(h, ROWS, stride=8), :] for t in range(LATENT // 128)]
            rows = jnp.concatenate(rows, axis=1).astype(BF16)
            values[j, n, :, h * 128 : h * 128 + 128] = dot(rows, wuv[h]).astype(BF16)
        yield from gather8(values.at[j], node, sems, here)
        if j == 0:
            loads[3].wait()
        product = dot(values[j].reshape(BATCH, 1024), wout[...]).astype(BF16)
        if j == 1:
            pick = select(DEVS, DEVS, lambda row, column: dest_v[...] == row)
            by_step = product.reshape(NODES, STEPS, LOCALS, COLS)
            moved = [dot(pick, by_step[:, s].reshape(DEVS, COLS)).astype(BF16) for s in range(STEPS)]
            moved = [m.reshape(NODES, LOCALS, COLS) for m in moved]
            product = jnp.concatenate(moved, axis=1)
        yield from halves(product, part, pair, summed, j, sems)
        yield from scatter8(
            summed.at[j], chips, sems, here, lambda: None, *[r.at[j] for r in attn_bufs]
        )
        if j == 0:
            loads[4].wait()
        slot = slots(LOCALS, lambda row: chip * LOCALS + row)
        pick = select(
            LOCALS, 2 * LOCALS,
            lambda row, column: (column // 2 == row) & ((lax.rem(column, 2) == slot) == (j == 1)),
        )
        skip = [dot(pick, resid[s, :, pl.ds(mine, HALF)]) for s in range(STEPS)]
        mixed[j, core, chip] = (jnp.concatenate(skip, axis=0) + total(attn_bufs, summed, chips, j)).astype(BF16)

        side = sems.take(8)
        side_ref = sems.ref.at[pl.ds(sems.used - 8, 8)]

        def on(block):
            ref = mixed.at[j, core, block]
            sems.start(ref, ref, side_ref.at[block], sibling)

        yield from gather8(mixed.at[j, core], chips, sems, here, on)
        for block in range(NODES):
            arrived(mixed.at[j, 1 - core, block], side[block], here)

        if j == 0:
            loads[5].wait()
            loads[6].wait()

        sq = sems.take(2)

        def expand(plane):
            at = pl.ds(plane * 4, 4)
            left = mixed[j, 0, at].reshape(4 * ROWS, HALF).astype(F32)
            right = mixed[j, 1, at, :, HALF - OFFSET :].reshape(4 * ROWS, OFFSET).astype(F32)
            rows = jnp.concatenate([left, right], axis=1)
            scaled = (rows * gain[...]).astype(BF16)
            square = rows * rows
            lanes = square[:, :128]
            for t in range(1, COLS // 128):
                lanes += square[:, t * 128 : t * 128 + 128]
            gu[j, at, :, :HID] = dot(scaled, wg[...]).astype(BF16).reshape(4, ROWS, HID)
            gu[j, at, :, HID:] = dot(scaled, wu[...]).astype(BF16).reshape(4, ROWS, HID)
            for k in range(4):
                to = plane * 4 + k
                sums = lax.dot_general(
                    jnp.ones((8, 128), F32), lanes[k * ROWS : (k + 1) * ROWS], NT,
                    precision=lax.Precision.HIGHEST, preferred_element_type=F32,
                )
                sq_send[j, to] = jnp.concatenate([sums, jnp.zeros((8, 128 - ROWS), F32)], axis=1)

        def own_plane():
            expand(node.p)

            def send_sq(i, c):
                p = lax.rem(n + i, NODES)
                rcopy(sq_send.at[j, p], sq_recv.at[j, n], sq[0], sq[1], (p, l)).start()
                return c

            lax.fori_loop(1, NODES, send_sq, 0)
            sq_recv[j, n] = sq_send[j, n]

        expand(node.q)
        yield from scatter8(gu.at[j], node, sems, here, own_plane, *[r.at[j] for r in gu_bufs])
        seven = pl.ds(0, NODES - 1)
        rcopy(sq_send.at[j, seven], sq_recv.at[j, seven], sq[0], sq[1], here).wait()
        inverse = lax.rsqrt(jnp.sum(sq_recv[j], axis=0) / D + EPS)
        inverse = jnp.broadcast_to(inverse[:1], (ROWS, 128))
        inverse = jnp.where(iota((ROWS, 128), 0) == iota((ROWS, 128), 1), inverse, 0.0)
        inverse = jnp.sum(inverse, axis=1, keepdims=True)
        summed_gu = total(gu_bufs, gu, node, j) * inverse
        gate, up = summed_gu[:, :HID], summed_gu[:, HID:]
        hidden[j, n] = (gate / (1.0 + jnp.exp(-gate)) * up).astype(BF16)
        yield from gather8(hidden.at[j], node, sems, here)
        if j == 0:
            loads[7].wait()
        product = dot(hidden[j].reshape(BATCH, HID), wd[...]).astype(BF16)
        yield from halves(product, part2, pair2, summed2, j, sems)
        yield from scatter8(
            summed2.at[j], chips, sems, here, lambda: None, *[r.at[j] for r in down_bufs]
        )
        last[j, core] = (mixed[j, core, chip].astype(F32) + total(down_bufs, summed2, chips, j)).astype(BF16)
        recv = sems.take(1)[0]
        sems.start(last.at[j, core], last.at[j, core], recv, sibling)
        yield
        arrived(last.at[j, 1 - core], recv, here)

    sems = [Sems(ref_a), Sems(ref_b)]
    attention(0)
    context = send_context(0, sems[0])

    both = pl.ds(0, DEVS - 1)
    rcopy(tiles.at[both], r1.at[both], far.at[0], far.at[1], here).wait()

    def sort(o, c):
        s2[o] = r1[dest_s[o]]
        return c

    lax.fori_loop(0, DEVS, sort, 0)

    def deliver(i, c):
        p = lax.rem(me + i, DEVS)
        rcopy(s2.at[p], r2.at[me], far.at[2], far.at[3], (p // LOCALS, lax.rem(p, LOCALS))).start()
        return c

    lax.fori_loop(1, DEVS, deliver, 0)
    r2[me] = s2[me]

    first = chain(0, sems[0], context)
    for _ in range(LEAD):
        next(first)
    rcopy(s2.at[both], r2.at[both], far.at[2], far.at[3], here).wait()
    for s in range(STEPS):
        for hb in range(blocks):
            for cb in range(5):
                query_arr[s * HEADS + hb * 16 : s * HEADS + hb * 16 + 16, cb * 128 : cb * 128 + 128] = r2[
                    (s * blocks + hb) * 5 + cb
                ]
    for cb in range(5):
        fresh[1, :, cb * 128 : cb * 128 + 128] = r2[STEPS * blocks * 5 + cb]
    attention(1)
    context = send_context(1, sems[1])
    next(first, None)
    chains = [chain(1, sems[1], context), first]
    while chains:
        for steps in list(chains):
            try:
                next(steps)
            except StopIteration:
                chains.remove(steps)

    slot = slots(LOCALS, lambda row: chip * LOCALS + core * 8 + row // 2)
    pick = select(
        LOCALS, LOCALS,
        lambda row, column: (lax.rem(column, 8) == row // 2) & ((lax.rem(row, 2) == slot) == (column >= 8)),
    )
    at = pl.multiple_of(core * 8, 8)
    for j in range(2):
        done[j, :, :HALF] = last[j, 0].astype(F32)
        done[j, :, HALF:] = last[j, 1, :, HALF - OFFSET :].astype(F32)
    for s in range(STEPS):
        rows = jnp.concatenate([done[j, pl.ds(s * LOCALS + at, 8), :] for j in range(2)], axis=0).astype(BF16)
        out[s] = dot(pick, rows).astype(BF16)
    for one in sems:
        for copy in one.sent:
            copy.wait_send()


LEAD = 2


def local(
    cache_pool, block_table, lengths, mig_slot, mig_dest, queries, new_entries, residual,
    w_uv, w_out, norm_gain, w_gate, w_up, w_down,
):
    by_slot = queries.reshape(STEPS * 2, HEADS, WIDTH)
    vm = pl.BlockSpec(memory_space=pltpu.VMEM)
    hbm = pl.BlockSpec(memory_space=pl.ANY)
    smem = pl.BlockSpec(memory_space=pltpu.SMEM)
    dma = pltpu.SemaphoreType.DMA
    V = pltpu.VMEM
    tile = (DEVS, 16, 128)
    return pl.pallas_call(
        kernel,
        out_shape=jax.ShapeDtypeStruct((STEPS, LOCALS, COLS), BF16),
        in_specs=[smem] * 4 + [vm] * 4 + [hbm] * 8,
        out_specs=vm,
        scratch_shapes=[
            V((STEPS * 2, HEADS, WIDTH), BF16), V((4, WIDTH, 256), BF16), V((STEPS, 32, COLS), BF16),
            V((8, LATENT, 128), BF16), V((1024, COLS), BF16), V((COLS, HID), BF16), V((COLS, HID), BF16),
            V((HID, COLS), BF16),
            V(tile, BF16), V(tile, BF16), V(tile, BF16), V(tile, BF16),
            V((STEPS * HEADS, KEYS), BF16), V((2, 16, KEYS), BF16),
            V((2, STEPS * HEADS, LATENT), F32),
            V((2, LOCALS, ROWS, 256), BF16), V((2, LOCALS, ROWS, 256), BF16),
            V((LATENT // 128, BATCH, 128), F32),
            V((2, NODES, ROWS, 1024), BF16), V((2, NODES, ROWS, COLS), BF16),
            V((2, NODES, ROWS, HALF), BF16), V((2, NODES, ROWS, HALF), BF16),
            V((2, 2, NODES, ROWS, HALF), BF16),
            *scatter8_shapes(HALF),
            V((2, NODES, ROWS, 2 * HID), BF16), V((2, NODES, 8, 128), F32), V((2, NODES, 8, 128), F32),
            V((2, NODES, ROWS, HID), BF16),
            *scatter8_shapes(2 * HID),
            V((2, NODES, ROWS, COLS), BF16), V((2, NODES, ROWS, HALF), BF16), V((2, NODES, ROWS, HALF), BF16),
            V((2, 2, ROWS, HALF), BF16), V((2, ROWS, COLS), F32),
            *scatter8_shapes(HALF),
            dma((8,)), pltpu.SemaphoreType.REGULAR, dma((4,)), dma((160,)), dma((160,)),
        ],
        compiler_params=pltpu.CompilerParams(
            collective_id=0, has_side_effects=True, vmem_limit_bytes=60 * 2**20
        ),
        name="layer",
    )(
        block_table, lengths, mig_slot, mig_dest, mig_slot.reshape(1, DEVS), mig_dest.reshape(1, DEVS),
        norm_gain.reshape(1, COLS), new_entries,
        by_slot, cache_pool, residual, w_uv, w_out, w_gate, w_up, w_down,
    )


def solution(mesh):
    in_specs = (
        P(("node", "local"), None, None),
        P(("node", "local"), None),
        P(),
        P(),
        P(),
        P(None, ("node", "local"), None),
        P(None, ("node", "local"), None),
        P(None, None, "node"),
        P("local", None, None),
        P("local", "node"),
        P("node"),
        P("node", "local"),
        P("node", "local"),
        P("local", "node"),
    )
    out_specs = P(None, "local", "node")
    return jax.shard_map(local, mesh=mesh, in_specs=in_specs, out_specs=out_specs, check_vma=False)
```

time: 889 us -> 149 us (0.17)
  waiting for transfers between devices: 622 us -> 0 us
  Pallas kernels: 0 us -> 143 us
  blocking collectives: 100 us -> 0 us
  starting transfers between devices: 41.1 us -> 0 us
  matrix products: 40.5 us -> 0 us
  local copies, waits for them, and re-layouts: 35.4 us -> 6.22 us
  other arithmetic: 24.2 us -> 0 us
  between operations: 23 us -> 0.01 us
    psum x2 -> x0, waiting for transfers between devices: 251 us -> none  [the longest x1 154 us: local(): lax.psum(partial_value.astype(jnp.bfloat16), 'local').astype(jnp.float32)]
    all_to_all x5 -> x0, waiting for transfers between devices: 187 us -> none  [the longest x1 130 us: local(): lax.all_to_all(onward, 'local', split_axis=0, concat_axis=0, tiled=True)]
    reduce_scatter x3 -> x0, waiting for transfers between devices: 183 us -> none  [local(): lax.psum_scatter(jnp.dot(hidden, w_down, preferred_element_type=jnp.float...]
    pallas_call x0 -> x1, Pallas kernels: none -> 143 us  [local(): pl.pallas_call(kernel, out_shape=jax.ShapeDtypeStruct((STEPS, LOCALS, COL...]
    all_gather x3 -> x0, blocking collectives: 85.5 us -> none  [local(): lax.all_gather(values, 'node', axis=0, tiled=True)]
    all_to_all x5 -> x0, starting transfers between devices: 40.9 us -> none  [the longest x3 26.2 us: local(): lax.all_to_all(contexts[step_index], 'local', split_axis=1, concat_axis=0...]
    dot_general x26 -> x0, matrix products: 40.5 us -> none  [the longest x3 10.5 us: local(): jnp.dot(hidden, w_down, preferred_element_type=jnp.float32)]
    psum x1 -> x0, blocking collectives: 14.9 us -> none  [local(): squares = lax.psum(jnp.sum(mixed_wide * mixed_wide, axis=1), 'node')]
  transfers between devices with their start and end apart: 10 -> 0, of which waited for: 8 -> 0; matrix products, arithmetic and copies ran while one was open for 5% -> 0% of each run, Pallas kernels for 0% -> 0%
where the time goes in v2:
time: 149 us
  Pallas kernels  143 us (96%)
  local copies, waits for them, and re-layouts  6.22 us (4%)
    pallas_call x1, Pallas kernels, local(): pl.pallas_call(kernel, out_shape=jax.ShapeDtypeStruct((STEPS, LOCALS, COL...  143 us
    reshape x1, local copies, waits for them, and re-layouts, local(): by_slot = queries.reshape(STEPS * 2, HEADS, WIDTH)  3.42 us

profile of v2, /device:TPU:1, one launch (start us, length us, event | category | flops | bytes accessed | tf_op | source)
XLA Modules:
  0.0 148.8 jit_solution(5586699938996078588)
XLA Ops:
  0.0 1.3 reshape.14.gain
  1.3 3.4 %reshape.15.query_hbm = bf16[6,128,576]{2,1,0:T(8,128)(2,1)} reshape(bf16[3,2,73728]{2,1,0:T(2,128)(2,1)} %param.19) | data formatting | bytes 1769472 | tf_op jit(solution)/shard_map/reshape | solution.py:514
  4.7 142.5 %layer.1 = bf16[3,16,896]{2,1,0:T(8,128)(2,1)} custom-call(s32[2,2]{1,0:T(2,128)} %table.1, s32[256]{0:T(256)} %lengths.1, s32[128]{0:T(128)} %slot_s.1, s32[128]{0:T(128)} %dest_s.1, s32[1,128]{1,0:T(1,128)} %bitcast.2, s32[1,128]{1,0:T(1,128)} %bitcast.3, f32[1,896]{1,0:T(1,128)} %reshape.14.gain, bf16[3,2,576]{2,1,0:T(2,128)(2,1)} %fresh_all.1, ...), custom_call_target="tpu_custom_call" | custom-call | tf_op jit(solution)/shard_map/layer/pallas_call | solution.py:521
  147.2 1.5 %copy.16 = bf16[3,16,896]{2,1,0:T(8,128)(2,1)} copy(bf16[3,16,896]{2,1,0:T(8,128)(2,1)} %layer.1) | data formatting | bytes 172032

commit v3 on v2

v3 whole, which is shorter than its diff:
```python
import jax
import jax.numpy as jnp
from jax import lax
from jax.experimental import pallas as pl
from jax.experimental.pallas import tpu as pltpu
from jax.sharding import PartitionSpec as P

MESH = pl.DeviceIdType.MESH
BF16, F32 = jnp.bfloat16, jnp.float32
D = 7168
QK_NOPE = 128
LATENT = 512
ROPE = 64
WIDTH = LATENT + ROPE
STEPS = 3
HEADS = 128
NODES, LOCALS = 8, 16
DEVS = NODES * LOCALS
EPS = 1e-06
SCALE = (QK_NOPE + ROPE) ** (-0.5)
COLS = 896
HALF = 512
OFFSET = COLS - HALF
HID = 1152
KEYS = 640
NT = (((1,), (1,)), ((), ()))


def dot(a, b):
    return jnp.dot(a, b, preferred_element_type=F32)


def dot_nt(a, b):
    return lax.dot_general(a, b, NT, preferred_element_type=F32)


def iota(shape, dim):
    return lax.broadcasted_iota(jnp.int32, shape, dim)


def rcopy(src, dst, send, recv, device):
    return pltpu.make_async_remote_copy(
        src_ref=src, dst_ref=dst, send_sem=send, recv_sem=recv, device_id=device, device_id_type=MESH
    )


def attend(query, fresh, key0, key1, length):
    s0 = dot(query, key0) * SCALE
    s1 = dot(query, key1) * SCALE
    sf = dot_nt(query, fresh) * SCALE
    rows, block = s0.shape
    column = iota((rows, block), 1)
    s0 = jnp.where(column < length, s0, -jnp.inf)
    s1 = jnp.where(column + block < length, s1, -jnp.inf)
    step = iota(sf.shape, 0) // HEADS
    sf = jnp.where(iota(sf.shape, 1) <= step, sf, -jnp.inf)
    top = jnp.maximum(
        jnp.max(jnp.maximum(s0, s1), axis=1, keepdims=True), jnp.max(sf, axis=1, keepdims=True)
    )
    w0 = jnp.exp(s0 - top)
    w1 = jnp.exp(s1 - top)
    wf = jnp.exp(sf - top)
    total = jnp.sum(w0 + w1, axis=1, keepdims=True) + jnp.sum(wf, axis=1, keepdims=True)
    context = dot_nt(w0.astype(BF16), key0[:LATENT])
    context += dot_nt(w1.astype(BF16), key1[:LATENT])
    context += dot(wf.astype(BF16), fresh[:, :LATENT])
    return context / total


class Group:
    def __init__(self, pair, ring, block, device):
        self.p, self.r = pair, ring
        self.q = 1 - pair
        self.up, self.dn, self.op = lax.rem(ring + 1, 4), lax.rem(ring + 3, 4), lax.rem(ring + 2, 4)
        self.block, self.device = block, device


class Pool:
    def __init__(self, ref):
        self.ref, self.free, self.used = ref, [], 0

    def take(self):
        if self.free:
            return self.free.pop()
        self.used += 1
        return self.used - 1


class Sems:
    def __init__(self, ref, pool):
        self.ref, self.pool, self.used, self.sent, self.older = ref, pool, 0, [], []

    def take(self, count):
        first = self.used
        self.used += count
        return [self.ref.at[first + i] for i in range(count)]

    def sender(self):
        index = self.pool.take()
        return index, self.pool.ref.at[index]

    def keep(self, index, copy):
        self.sent.append((index, copy))

    def start(self, src, dst, recv, device):
        index, send = self.sender()
        copy = rcopy(src, dst, send, recv, device)
        copy.start()
        self.keep(index, copy)

    def settle(self):
        for index, copy in self.older:
            copy.wait_send()
            self.pool.free.append(index)
        self.older, self.sent = self.sent, []


def arrived(ref, recv, here):
    rcopy(ref, ref, recv, recv, here).wait_recv()


def gather8(buf, g, sems, here):
    width = buf.shape[-1] // 256 * 128
    lo, hi = pl.ds(0, width), pl.ds(width, buf.shape[-1] - width)
    recv = sems.take(5)
    b = g.block

    def send(block, to, index, cols=None):
        ref = buf.at[block] if cols is None else buf.at[block, :, cols]
        sems.start(ref, ref, recv[index], g.device(*to))

    own = b(g.p, g.r)
    send(own, (g.p, g.up), 1)
    send(own, (g.p, g.dn), 0)
    send(own, (g.q, g.r), 2)
    yield
    arrived(buf.at[b(g.p, g.up)], recv[0], here)
    send(b(g.p, g.up), (g.p, g.dn), 3, lo)
    arrived(buf.at[b(g.p, g.dn)], recv[1], here)
    send(b(g.p, g.dn), (g.p, g.up), 3, hi)
    arrived(buf.at[b(g.q, g.r)], recv[2], here)
    send(b(g.q, g.r), (g.p, g.up), 4)
    send(b(g.q, g.r), (g.p, g.dn), 4)
    yield
    arrived(buf.at[b(g.p, g.op)], recv[3], here)
    send(b(g.p, g.op), (g.q, g.r), 4)
    yield
    arrived(buf.at[pl.ds(0, 3)], recv[4], here)


def scatter8(part, g, sems, here, meanwhile, ra, rb, rc, rd, re, sc, sd, se):
    width = part.shape[-1] // 2
    halves = (pl.ds(0, width), pl.ds(width, width))
    recv = sems.take(5)
    b = g.block

    def wide(ref, *at):
        return ref[at].astype(F32)

    sems.start(part.at[b(g.q, g.op)], ra, recv[0], g.device(g.q, g.r))
    sems.start(part.at[b(g.q, g.up)], rb.at[0], recv[1], g.device(g.p, g.up))
    sems.start(part.at[b(g.q, g.dn)], rb.at[1], recv[1], g.device(g.p, g.dn))
    meanwhile()
    up, dn = b(g.p, g.up), b(g.p, g.dn)
    yield
    arrived(ra, recv[0], here)
    sc[...] = (wide(part, b(g.p, g.op)) + wide(ra, ...)).astype(BF16)
    sems.start(sc.at[:, halves[0]], rc.at[0], recv[2], g.device(g.p, g.up))
    sems.start(sc.at[:, halves[1]], rc.at[1], recv[2], g.device(g.p, g.dn))
    sems.start(part.at[up, :, halves[1]], re.at[0, :, halves[1]], recv[4], g.device(g.p, g.up))
    sems.start(part.at[dn, :, halves[0]], re.at[1, :, halves[0]], recv[4], g.device(g.p, g.dn))
    arrived(rb, recv[1], here)
    sd[...] = (wide(part, b(g.q, g.r)) + wide(rb, 0) + wide(rb, 1)).astype(BF16)
    sems.start(sd, rd, recv[3], g.device(g.q, g.r))
    yield
    arrived(rc, recv[2], here)
    se[0] = (wide(part, up, slice(None), halves[0]) + wide(rc, 0)).astype(BF16)
    sems.start(se.at[0], re.at[0, :, halves[0]], recv[4], g.device(g.p, g.up))
    se[1] = (wide(part, dn, slice(None), halves[1]) + wide(rc, 1)).astype(BF16)
    sems.start(se.at[1], re.at[1, :, halves[1]], recv[4], g.device(g.p, g.dn))
    yield
    arrived(rd, recv[3], here)
    arrived(re, recv[4], here)


def ring_scatter(part, got, away, g, sems, here):
    recv = sems.take(1)[0]
    for i, ring in enumerate((g.up, g.dn, g.op)):
        sems.start(part.at[pl.ds(ring * 2, 2)], got.at[i], recv, g.device(g.p, ring))
    yield
    arrived(got, recv, here)
    terms = [part[pl.ds(g.r * 2, 2)]] + [got[i] for i in range(3)]
    away[...] = sum(t.astype(F32) for t in terms).astype(BF16)


def scatter1(part, got, own, device, sems, here):
    recv = sems.take(1)[0]
    index, send = sems.sender()

    def spread(i, c):
        to = lax.rem(own + i, 8)
        rcopy(part.at[to], got.at[own], send, recv, device(to)).start()
        return c

    lax.fori_loop(1, 8, spread, 0)
    got[own] = part[own]
    seven = pl.ds(0, 7)
    sems.keep(index, rcopy(part.at[seven], got.at[seven], send, recv, here))
    yield
    rcopy(part.at[seven], got.at[seven], send, recv, here).wait_recv()


def ring_shapes(rows, cols):
    V = pltpu.VMEM
    return [V((3, 2, rows, cols), BF16), V((2, rows, cols), BF16), V((2, rows, cols), BF16)]


def scatter8_shapes(rows, cols):
    V = pltpu.VMEM
    return [
        V((rows, cols), BF16), V((2, rows, cols), BF16), V((2, rows, cols // 2), BF16),
        V((rows, cols), BF16), V((2, rows, cols), BF16), V((rows, cols), BF16),
        V((rows, cols), BF16), V((2, rows, cols // 2), BF16),
    ]


def chain_shapes(steps):
    V = pltpu.VMEM
    rows = LOCALS * steps
    return [
        V((LOCALS, rows, 256), BF16), V((LOCALS, rows, 256), BF16), V((LATENT // 128, 8 * rows, 128), F32),
        V((NODES, rows, 1024), BF16), V((NODES, rows, COLS), BF16),
        V((NODES, rows, HALF), BF16), V((NODES, rows, HALF), BF16), V((2, NODES, rows, HALF), BF16),
        *ring_shapes(rows, HALF),
        V((NODES, rows, 2 * HID), BF16), V((8, NODES * rows), F32), V((NODES, 8, NODES * rows), F32),
        V((NODES, rows, HID), BF16),
        *scatter8_shapes(rows, 2 * HID),
        V((NODES, rows, COLS), BF16), V((NODES, rows, HALF), BF16), V((NODES, rows, HALF), BF16),
        V((NODES, rows, HALF), BF16), V((2, rows, HALF), BF16), V((rows, COLS), F32),
    ]


def kernel(
    table, lengths, slot_s, dest_s, slot_v, dest_v, gain, fresh_all,
    query_hbm, pool_hbm, resid_hbm, wuv_hbm, wout_hbm, wg_hbm, wu_hbm, wd_hbm,
    out, *scratch,
):
    refs = list(scratch)
    take = lambda count=1: [refs.pop(0) for _ in range(count)]
    query, pool, resid, wuv, wout, wg, wu, wd = take(8)
    tiles, r1, s2, r2, query_arr, fresh, ctx = take(7)
    bufs = [take(len(chain_shapes(1))) for _ in CHAINS]
    wsem, ready, far, senders = take(4)
    senders = Pool(senders)
    sems = [Sems(ref, senders) for ref in take(len(CHAINS))]

    n, l = lax.axis_index("node"), lax.axis_index("local")
    me = n * LOCALS + l
    here = (n, l)
    core, chip = lax.rem(l, 2), l // 2
    sibling = (n, l + 1 - 2 * core)
    mine = pl.multiple_of(core * OFFSET, 128)
    theirs = pl.multiple_of((1 - core) * OFFSET, 128)
    node = Group(n // 4, lax.rem(n, 4), lambda p, r: p * 4 + r, lambda p, r: (p * 4 + r, l))
    chips = Group(
        lax.rem(chip, 2), chip // 2, lambda p, r: r * 2 + p, lambda p, r: (n, (r * 2 + p) * 2 + core)
    )

    barrier = pltpu.get_barrier_semaphore()

    def greet_node(i, c):
        pl.semaphore_signal(barrier, inc=1, device_id=(lax.rem(n + i, NODES), l), device_id_type=MESH)
        return c

    def greet_local(i, c):
        pl.semaphore_signal(barrier, inc=1, device_id=(n, lax.rem(l + i, LOCALS)), device_id_type=MESH)
        return c

    def greet_all(i, c):
        pl.semaphore_signal(ready, inc=1, device_id=(n, lax.rem(l + i, LOCALS)), device_id_type=MESH)
        return c

    lax.fori_loop(1, NODES, greet_node, 0)
    lax.fori_loop(1, LOCALS, greet_local, 0)

    loads = [
        pltpu.make_async_copy(a, b, wsem.at[i])
        for i, (a, b) in enumerate(
            (
                (query_hbm, query), (pool_hbm, pool), (wuv_hbm, wuv), (wout_hbm, wout),
                (resid_hbm.at[:, pl.ds(chip // 2 * 64, 64), :], resid),
                (wg_hbm, wg), (wu_hbm, wu), (wd_hbm, wd),
            )
        )
    ]
    for copy in loads:
        copy.start()

    gain_row = gain[...].reshape(1, COLS)
    leave = slot_s[me]
    stay = 1 - leave

    fresh[...] = jnp.zeros(fresh.shape, BF16)
    both_fresh = fresh_all[...].astype(F32)
    fresh[0, :STEPS, :WIDTH] = jnp.where(stay == 0, both_fresh[:, 0], both_fresh[:, 1]).astype(BF16)
    fresh[1, :STEPS, :WIDTH] = jnp.where(stay == 1, both_fresh[:, 0], both_fresh[:, 1]).astype(BF16)
    loads[0].wait()
    blocks = HEADS // 16
    for s in range(STEPS):
        for hb in range(blocks):
            for cb in range(5):
                width = min(128, WIDTH - cb * 128)
                tiles[(s * blocks + hb) * 5 + cb, :, :width] = query[
                    s * 2 + leave, hb * 16 : hb * 16 + 16, cb * 128 : cb * 128 + width
                ]
    for cb in range(5):
        tiles[STEPS * blocks * 5 + cb] = fresh[1, :, cb * 128 : cb * 128 + 128]

    def spread(i, c):
        p = lax.rem(me + i, DEVS)
        rcopy(tiles.at[p], r1.at[me], far.at[0], far.at[1], (p // LOCALS, lax.rem(p, LOCALS))).start()
        return c

    r1[me] = tiles[me]

    def attention(j):
        if j == 0:
            request, new = stay, fresh[0, :, :WIDTH]
            rows = jnp.concatenate([query[s * 2 + stay] for s in range(STEPS)], axis=0)
        else:
            request, new = leave, fresh[1, :, :WIDTH]
            rows = query_arr[:, :WIDTH]
        key0, key1 = pool[table[request, 0]], pool[table[request, 1]]
        ctx[j] = attend(rows, new, key0, key1, lengths[me * 2 + request])

    others = pl.ds(0, LOCALS - 1)

    def send_context(j, steps, bufs, sems):
        ctx_send, ctx_recv = bufs[:2]

        def group(g):
            at = pl.multiple_of(g * 8, 8)
            rows = jnp.concatenate([ctx[j, pl.ds(s * HEADS + at, 8), :] for s in steps], axis=0)
            return jnp.concatenate([rows[:, :256], rows[:, 256:]], axis=0).astype(BF16)

        send, recv = sems.take(2)

        def send_group(i, c):
            g = lax.rem(l + i, LOCALS)
            ctx_send[g] = group(g)
            rcopy(ctx_send.at[g], ctx_recv.at[l], send, recv, (n, g)).start()
            return c

        lax.fori_loop(1, LOCALS, send_group, 0)
        ctx_recv[l] = group(l)
        return rcopy(ctx_send.at[others], ctx_recv.at[others], send, recv, here)

    def select(rows, columns, test):
        return jnp.where(test(iota((rows, columns), 0), iota((rows, columns), 1)), 1.0, 0.0).astype(BF16)

    def slots(rows, device):
        lanes = jnp.broadcast_to(slot_v[...], (rows, DEVS)).astype(F32)
        at = device(iota((rows, DEVS), 0)) == iota((rows, DEVS), 1)
        return jnp.sum(jnp.where(at, lanes, 0.0), axis=1, keepdims=True).astype(jnp.int32)

    def chain(j, steps, bufs, sems, context, only):
        count = len(steps)
        rows = LOCALS * count
        bufs = list(bufs)
        take = lambda count=1: [bufs.pop(0) for _ in range(count)]
        ctx_send, ctx_recv, wide, values, part, pair, summed, mixed = take(8)
        got, away, back = take(3)
        gu, sq_send, sq_recv, hidden = take(4)
        gu_bufs = take(8)
        part2, pair2, summed2 = take(3)
        got2 = take()[0]
        last, done = take(2)

        def halves(product, part, pair, summed):
            part[...] = product.reshape(NODES, rows, COLS)
            recv = sems.take(1)[0]
            sems.start(part.at[:, :, pl.ds(theirs, HALF)], pair, recv, sibling)
            yield
            arrived(pair, recv, here)
            summed[...] = (part[:, :, pl.ds(mine, HALF)].astype(F32) + pair[...].astype(F32)).astype(BF16)

        if only:
            loads[2].wait()
        context.wait()
        for t in range(2):
            recv = ctx_recv[:, :, t * 128 : t * 128 + 128].astype(F32)
            for half in range(2):
                for s in range(count):
                    at = (half * count + s) * 8
                    wide[half * 2 + t, s * 128 : s * 128 + 128] = recv[:, at : at + 8].reshape(128, 128)
        for h in range(8):
            head = [wide[t, pl.ds(h, rows, stride=8), :] for t in range(LATENT // 128)]
            head = jnp.concatenate(head, axis=1).astype(BF16)
            values[n, :, h * 128 : h * 128 + 128] = dot(head, wuv[h]).astype(BF16)
        yield from gather8(values, node, sems, here)
        if only:
            loads[3].wait()
        product = dot(values[...].reshape(NODES * rows, 1024), wout[...]).astype(BF16)
        if j == 1:
            pick = select(DEVS, DEVS, lambda row, column: dest_v[...] == row)
            by_step = product.reshape(NODES, count, LOCALS, COLS)
            moved = [dot(pick, by_step[:, s].reshape(DEVS, COLS)).astype(BF16) for s in range(count)]
            product = jnp.concatenate([m.reshape(NODES, LOCALS, COLS) for m in moved], axis=1)
        yield from halves(product, part, pair, summed)

        yield from ring_scatter(summed, got, away, chips, sems, here)
        recv = sems.take(1)[0]
        sems.start(away, back, recv, chips.device(chips.q, chips.r))
        if only:
            loads[4].wait()
        slot = slots(2 * LOCALS, lambda row: chips.r * 2 * LOCALS + row)
        pick = select(
            2 * LOCALS, 4 * LOCALS,
            lambda row, column: (column // 2 == row) & ((lax.rem(column, 2) == slot) == (j == 1)),
        )
        skip = [dot(pick, resid[s, :, pl.ds(mine, HALF)]) for s in steps]
        skip = jnp.concatenate([k.reshape(2, LOCALS, HALF) for k in skip], axis=1)
        yield
        arrived(back, recv, here)
        two = pl.ds(chips.r * 2, 2)
        mixed[core, two] = (skip + (away[...].astype(F32) + back[...].astype(F32))).astype(BF16)

        side = sems.take(1)[0]
        recv = sems.take(3)

        def pass_on(ring):
            ref = mixed.at[core, pl.ds(ring * 2, 2)]
            sems.start(ref, ref, side, sibling)

        for i, ring in enumerate((chips.up, chips.dn, chips.op)):
            ref = mixed.at[core, two]
            sems.start(ref, ref, recv[i], chips.device(chips.p, ring))
        pass_on(chips.r)
        yield
        for i, ring in enumerate((chips.dn, chips.up, chips.op)):
            arrived(mixed.at[core, pl.ds(ring * 2, 2)], recv[i], here)
            pass_on(ring)
        arrived(mixed.at[1 - core], side, here)

        if only:
            loads[5].wait()
            loads[6].wait()
        sq = sems.take(2)

        left = mixed[0].reshape(NODES * rows, HALF).astype(F32)
        right = mixed[1, :, :, HALF - OFFSET :].reshape(NODES * rows, OFFSET).astype(F32)
        whole = jnp.concatenate([left, right], axis=1)
        scaled = (whole * gain_row).astype(BF16)
        gu[:, :, :HID] = dot(scaled, wg[...]).astype(BF16).reshape(NODES, rows, HID)
        gu[:, :, HID:] = dot(scaled, wu[...]).astype(BF16).reshape(NODES, rows, HID)

        def squares():
            square = whole * whole
            lanes = square[:, :128]
            for t in range(1, COLS // 128):
                lanes += square[:, t * 128 : t * 128 + 128]
            sq_send[...] = lax.dot_general(
                jnp.ones((8, 128), F32), lanes, NT, precision=lax.Precision.HIGHEST, preferred_element_type=F32
            )

            def send_sq(i, c):
                p = lax.rem(n + i, NODES)
                rcopy(sq_send, sq_recv.at[n], sq[0], sq[1], (p, l)).start()
                return c

            lax.fori_loop(1, NODES, send_sq, 0)
            sq_recv[n] = sq_send[...]

        yield from scatter8(gu, node, sems, here, squares, *gu_bufs)
        seven = pl.ds(0, NODES - 1)
        rcopy(sq_recv.at[seven], sq_recv.at[seven], sq[0], sq[1], here).wait()
        inverse = lax.rsqrt(jnp.sum(sq_recv[...], axis=0) / D + EPS)
        inverse = jnp.broadcast_to(inverse[:1], (rows, NODES * rows))
        lane = n * rows + iota((rows, NODES * rows), 0)
        inverse = jnp.where(iota((rows, NODES * rows), 1) == lane, inverse, 0.0)
        inverse = jnp.sum(inverse, axis=1, keepdims=True)
        rd, re = gu_bufs[3], gu_bufs[4]
        total = gu[n].astype(F32) + rd[...].astype(F32) + re[0].astype(F32) + re[1].astype(F32)
        total *= inverse
        gate, up = total[:, :HID], total[:, HID:]
        hidden[n] = (gate / (1.0 + jnp.exp(-gate)) * up).astype(BF16)
        yield from gather8(hidden, node, sems, here)
        if only:
            loads[7].wait()
        product = dot(hidden[...].reshape(NODES * rows, HID), wd[...]).astype(BF16)
        yield from halves(product, part2, pair2, summed2)
        yield from scatter1(summed2, got2, chip, lambda to: (n, to * 2 + core), sems, here)
        total = jnp.sum(got2[...].astype(F32), axis=0)
        last[core] = (mixed[core, chip].astype(F32) + total).astype(BF16)
        recv = sems.take(1)[0]
        sems.start(last.at[core], last.at[core], recv, sibling)
        yield
        arrived(last.at[1 - core], recv, here)
        done[:, :HALF] = last[0].astype(F32)
        done[:, HALF:] = last[1, :, HALF - OFFSET :].astype(F32)

    both = pl.ds(0, DEVS - 1)
    running = {}

    def begin(j):
        for k, (which, steps) in enumerate(CHAINS):
            if which == j:
                context = send_context(j, steps, bufs[k], sems[k])
                running["abcdef"[k]] = (chain(j, steps, bufs[k], sems[k], context, k == 0), sems[k])

    def sort_tiles():
        rcopy(tiles.at[both], r1.at[both], far.at[0], far.at[1], here).wait()

        def sort(o, c):
            s2[o] = r1[dest_s[o]]
            return c

        lax.fori_loop(0, DEVS, sort, 0)

        def deliver(i, c):
            p = lax.rem(me + i, DEVS)
            rcopy(s2.at[p], r2.at[me], far.at[2], far.at[3], (p // LOCALS, lax.rem(p, LOCALS))).start()
            return c

        lax.fori_loop(1, DEVS, deliver, 0)
        r2[me] = s2[me]

    def attend_moved():
        rcopy(s2.at[both], r2.at[both], far.at[2], far.at[3], here).wait()
        for s in range(STEPS):
            for hb in range(blocks):
                for cb in range(5):
                    at = s * HEADS + hb * 16
                    query_arr[at : at + 16, cb * 128 : cb * 128 + 128] = r2[(s * blocks + hb) * 5 + cb]
        for cb in range(5):
            fresh[1, :, cb * 128 : cb * 128 + 128] = r2[STEPS * blocks * 5 + cb]
        attention(1)
        begin(1)

    loads[1].wait()
    attention(0)
    pl.semaphore_wait(barrier, NODES - 1 + LOCALS - 1)
    lax.fori_loop(1, LOCALS, greet_all, 0)
    begin(0)
    pl.semaphore_wait(ready, LOCALS - 1)
    lax.fori_loop(1, DEVS, spread, 0)

    def advance(name):
        steps, held = running[name]
        held.settle()
        try:
            next(steps)
        except StopIteration:
            del running[name]

    for name in ORDER:
        if name == "1":
            sort_tiles()
        elif name == "2":
            attend_moved()
        elif name in running:
            advance(name)
    while running:
        for name in list(running):
            advance(name)

    slot = slots(LOCALS, lambda row: chip * LOCALS + core * 8 + row // 2)
    pick = select(
        LOCALS, LOCALS,
        lambda row, column: (lax.rem(column, 8) == row // 2) & ((lax.rem(row, 2) == slot) == (column >= 8)),
    )
    at = pl.multiple_of(core * 8, 8)
    for s in range(STEPS):
        rows = [
            bufs[k][-1][pl.ds(steps.index(s) * LOCALS + at, 8), :]
            for j in range(2)
            for k, (which, steps) in enumerate(CHAINS)
            if which == j and s in steps
        ]
        out[s] = dot(pick, jnp.concatenate(rows, axis=0).astype(BF16)).astype(BF16)
    for held in sems:
        held.settle()
        held.settle()
        assert held.used <= RECEIVERS and senders.used <= SENDERS


CHAINS = ((0, (0,)), (0, (1, 2)), (1, (0,)), (1, (1, 2)))
SENDERS, RECEIVERS = 36, 29
ORDER = "ab1abab2ababcd"


def local(
    cache_pool, block_table, lengths, mig_slot, mig_dest, queries, new_entries, residual,
    w_uv, w_out, norm_gain, w_gate, w_up, w_down,
):
    by_slot = queries.reshape(STEPS * 2, HEADS, WIDTH)
    vm = pl.BlockSpec(memory_space=pltpu.VMEM)
    hbm = pl.BlockSpec(memory_space=pl.ANY)
    smem = pl.BlockSpec(memory_space=pltpu.SMEM)
    dma = pltpu.SemaphoreType.DMA
    V = pltpu.VMEM
    tile = (DEVS, 16, 128)
    return pl.pallas_call(
        kernel,
        out_shape=jax.ShapeDtypeStruct((STEPS, LOCALS, COLS), BF16),
        in_specs=[smem] * 4 + [vm] * 4 + [hbm] * 8,
        out_specs=vm,
        scratch_shapes=[
            V((STEPS * 2, HEADS, WIDTH), BF16), V((4, WIDTH, 256), BF16), V((STEPS, 64, COLS), BF16),
            V((8, LATENT, 128), BF16), V((1024, COLS), BF16), V((COLS, HID), BF16), V((COLS, HID), BF16),
            V((HID, COLS), BF16),
            V(tile, BF16), V(tile, BF16), V(tile, BF16), V(tile, BF16),
            V((STEPS * HEADS, KEYS), BF16), V((2, 16, KEYS), BF16), V((2, STEPS * HEADS, LATENT), F32),
            *[shape for _, steps in CHAINS for shape in chain_shapes(len(steps))],
            dma((8,)), pltpu.SemaphoreType.REGULAR, dma((4,)), dma((SENDERS,)), *[dma((RECEIVERS,)) for _ in CHAINS],
        ],
        compiler_params=pltpu.CompilerParams(
            collective_id=0, has_side_effects=True, vmem_limit_bytes=60 * 2**20
        ),
        name="layer",
    )(
        block_table, lengths, mig_slot, mig_dest, mig_slot.reshape(1, DEVS), mig_dest.reshape(1, DEVS),
        norm_gain, new_entries,
        by_slot, cache_pool, residual, w_uv, w_out, w_gate, w_up, w_down,
    )


def solution(mesh):
    in_specs = (
        P(("node", "local"), None, None),
        P(("node", "local"), None),
        P(),
        P(),
        P(),
        P(None, ("node", "local"), None),
        P(None, ("node", "local"), None),
        P(None, None, "node"),
        P("local", None, None),
        P("local", "node"),
        P("node"),
        P("node", "local"),
        P("node", "local"),
        P("local", "node"),
    )
    out_specs = P(None, "local", "node")
    return jax.shard_map(local, mesh=mesh, in_specs=in_specs, out_specs=out_specs, check_vma=False)
```

time: 149 us -> 129 us (0.87)
  Pallas kernels: 143 us -> 124 us
    pallas_call x1, Pallas kernels: 143 us -> 124 us  [local(): pl.pallas_call(kernel, out_shape=jax.ShapeDtypeStruct((STEPS, LOCALS, COL...]
where the time goes in v3:
time: 129 us
  Pallas kernels  124 us (96%)
  local copies, waits for them, and re-layouts  4.95 us (4%)
    pallas_call x1, Pallas kernels, local(): pl.pallas_call(kernel, out_shape=jax.ShapeDtypeStruct((STEPS, LOCALS, COL...  124 us
    reshape x1, local copies, waits for them, and re-layouts, local(): by_slot = queries.reshape(STEPS * 2, HEADS, WIDTH)  3.42 us

profile of v3, /device:TPU:1, one launch (start us, length us, event | category | flops | bytes accessed | tf_op | source)
XLA Modules:
  0.0 128.9 jit_solution(12975895817232494131)
XLA Ops:
  0.0 3.4 %reshape.11.query_hbm = bf16[6,128,576]{2,1,0:T(8,128)(2,1)} reshape(bf16[3,2,73728]{2,1,0:T(2,128)(2,1)} %param.19) | data formatting | bytes 1769472 | tf_op jit(solution)/shard_map/reshape | solution.py:596
  3.4 124.0 %layer.1 = bf16[3,16,896]{2,1,0:T(8,128)(2,1)} custom-call(s32[2,2]{1,0:T(2,128)} %table.1, s32[256]{0:T(256)} %lengths.1, s32[128]{0:T(128)} %slot_s.1, s32[128]{0:T(128)} %dest_s.1, s32[1,128]{1,0:T(1,128)} %bitcast.2, s32[1,128]{1,0:T(1,128)} %bitcast.3, f32[896]{0:T(1024)} %gain.1, bf16[3,2,576]{2,1,0:T(2,128)(2,1)} %fresh_all.1, ...), custom_call_target="tpu_custom_call" | custom-call | tf_op jit(solution)/shard_map/layer/pallas_call | solution.py:603
  127.4 1.5 %copy.16 = bf16[3,16,896]{2,1,0:T(8,128)(2,1)} copy(bf16[3,16,896]{2,1,0:T(8,128)(2,1)} %layer.1) | data formatting | bytes 172032

commit v4 on v3

--- a/solution.py
+++ b/solution.py
@@ -148,6 +148,26 @@
     arrived(buf.at[pl.ds(0, 3)], recv[4], here)
 
 
+def gather2(buf, g, sems, here):
+    recv = sems.take(3)
+    rings = (g.up, g.dn, g.op)
+
+    def send(block, index, *to):
+        sems.start(buf.at[block], buf.at[block], recv[index], g.device(*to))
+
+    own, other = g.block(g.p, g.r), g.block(g.q, g.r)
+    send(own, 0, g.q, g.r)
+    for ring in rings:
+        send(own, 1, g.p, ring)
+    yield
+    arrived(buf.at[other], recv[0], here)
+    for ring in rings:
+        send(other, 2, g.p, ring)
+    yield
+    arrived(buf.at[pl.ds(0, 3)], recv[1], here)
+    arrived(buf.at[pl.ds(0, 3)], recv[2], here)
+
+
 def scatter8(part, g, sems, here, meanwhile, ra, rb, rc, rd, re, sc, sd, se):
     width = part.shape[-1] // 2
     halves = (pl.ds(0, width), pl.ds(width, width))
@@ -397,7 +417,7 @@
             head = [wide[t, pl.ds(h, rows, stride=8), :] for t in range(LATENT // 128)]
             head = jnp.concatenate(head, axis=1).astype(BF16)
             values[n, :, h * 128 : h * 128 + 128] = dot(head, wuv[h]).astype(BF16)
-        yield from gather8(values, node, sems, here)
+        yield from GATHER[VALUES[j]](values, node, sems, here)
         if only:
             loads[3].wait()
         product = dot(values[...].reshape(NODES * rows, 1024), wout[...]).astype(BF16)
@@ -484,7 +504,7 @@
         total *= inverse
         gate, up = total[:, :HID], total[:, HID:]
         hidden[n] = (gate / (1.0 + jnp.exp(-gate)) * up).astype(BF16)
-        yield from gather8(hidden, node, sems, here)
+        yield from GATHER[HIDDEN[j]](hidden, node, sems, here)
         if only:
             loads[7].wait()
         product = dot(hidden[...].reshape(NODES * rows, HID), wd[...]).astype(BF16)
@@ -508,6 +528,14 @@
                 context = send_context(j, steps, bufs[k], sems[k])
                 running["abcdef"[k]] = (chain(j, steps, bufs[k], sems[k], context, k == 0), sems[k])
 
+    def advance(name):
+        steps, held = running[name]
+        held.settle()
+        try:
+            next(steps)
+        except StopIteration:
+            del running[name]
+
     def sort_tiles():
         rcopy(tiles.at[both], r1.at[both], far.at[0], far.at[1], here).wait()
 
@@ -544,14 +572,6 @@
     begin(0)
     pl.semaphore_wait(ready, LOCALS - 1)
     lax.fori_loop(1, DEVS, spread, 0)
-
-    def advance(name):
-        steps, held = running[name]
-        held.settle()
-        try:
-            next(steps)
-        except StopIteration:
-            del running[name]
 
     for name in ORDER:
         if name == "1":
@@ -584,9 +604,12 @@
         assert held.used <= RECEIVERS and senders.used <= SENDERS
 
 
-CHAINS = ((0, (0,)), (0, (1, 2)), (1, (0,)), (1, (1, 2)))
-SENDERS, RECEIVERS = 36, 29
-ORDER = "ab1abab2ababcd"
+CHAINS = ((0, (0,)), (0, (1,)), (0, (2,)), (1, (0,)), (1, (1,)), (1, (2,)))
+SENDERS, RECEIVERS = 51, 29
+GATHER = {"three": gather8, "two": gather2}
+VALUES = ("three", "three")
+HIDDEN = ("three", "two")
+ORDER = "abcabc1abc2abcabcdef"
 
 
 def local(

time: 129 us -> 125 us (0.969)
  Pallas kernels: 124 us -> 120 us
    pallas_call x1, Pallas kernels: 124 us -> 120 us  [local(): pl.pallas_call(kernel, out_shape=jax.ShapeDtypeStruct((STEPS, LOCALS, COL...]
where the time goes in v4:
time: 125 us
  Pallas kernels  120 us (96%)
  local copies, waits for them, and re-layouts  4.95 us (4%)
    pallas_call x1, Pallas kernels, local(): pl.pallas_call(kernel, out_shape=jax.ShapeDtypeStruct((STEPS, LOCALS, COL...  120 us
    reshape x1, local copies, waits for them, and re-layouts, local(): by_slot = queries.reshape(STEPS * 2, HEADS, WIDTH)  3.42 us

profile of v4, /device:TPU:1, one launch (start us, length us, event | category | flops | bytes accessed | tf_op | source)
XLA Modules:
  0.0 124.9 jit_solution(18177795006748492832)
XLA Ops:
  0.0 3.4 %reshape.11.query_hbm = bf16[6,128,576]{2,1,0:T(8,128)(2,1)} reshape(bf16[3,2,73728]{2,1,0:T(2,128)(2,1)} %param.19) | data formatting | bytes 1769472 | tf_op jit(solution)/shard_map/reshape | solution.py:619
  3.4 120.0 %layer.1 = bf16[3,16,896]{2,1,0:T(8,128)(2,1)} custom-call(s32[2,2]{1,0:T(2,128)} %table.1, s32[256]{0:T(256)} %lengths.1, s32[128]{0:T(128)} %slot_s.1, s32[128]{0:T(128)} %dest_s.1, s32[1,128]{1,0:T(1,128)} %bitcast.2, s32[1,128]{1,0:T(1,128)} %bitcast.3, f32[896]{0:T(1024)} %gain.1, bf16[3,2,576]{2,1,0:T(2,128)(2,1)} %fresh_all.1, ...), custom_call_target="tpu_custom_call" | custom-call | tf_op jit(solution)/shard_map/layer/pallas_call | solution.py:626
  123.4 1.5 %copy.16 = bf16[3,16,896]{2,1,0:T(8,128)(2,1)} copy(bf16[3,16,896]{2,1,0:T(8,128)(2,1)} %layer.1) | data formatting | bytes 172032

commit v5 on v4

--- a/solution.py
+++ b/solution.py
@@ -313,7 +313,7 @@
             )
         )
     ]
-    for copy in loads:
+    for copy in loads[:2]:
         copy.start()
 
     gain_row = gain[...].reshape(1, COLS)
@@ -566,6 +566,8 @@
         begin(1)
 
     loads[1].wait()
+    for copy in loads[2:]:
+        copy.start()
     attention(0)
     pl.semaphore_wait(barrier, NODES - 1 + LOCALS - 1)
     lax.fori_loop(1, LOCALS, greet_all, 0)

time: 125 us -> 125 us (level)
  no operation moved by 1% of the time
where the time goes in v5:
time: 125 us
  Pallas kernels  120 us (96%)
  local copies, waits for them, and re-layouts  4.95 us (4%)
    pallas_call x1, Pallas kernels, local(): pl.pallas_call(kernel, out_shape=jax.ShapeDtypeStruct((STEPS, LOCALS, COL...  120 us
    reshape x1, local copies, waits for them, and re-layouts, local(): by_slot = queries.reshape(STEPS * 2, HEADS, WIDTH)  3.42 us

profile of v5, /device:TPU:1, one launch (start us, length us, event | category | flops | bytes accessed | tf_op | source)
XLA Modules:
  0.0 124.9 jit_solution(13646169977857856758)
XLA Ops:
  0.0 3.4 %reshape.11.query_hbm = bf16[6,128,576]{2,1,0:T(8,128)(2,1)} reshape(bf16[3,2,73728]{2,1,0:T(2,128)(2,1)} %param.19) | data formatting | bytes 1769472 | tf_op jit(solution)/shard_map/reshape | solution.py:621
  3.4 120.0 %layer.1 = bf16[3,16,896]{2,1,0:T(8,128)(2,1)} custom-call(s32[2,2]{1,0:T(2,128)} %table.1, s32[256]{0:T(256)} %lengths.1, s32[128]{0:T(128)} %slot_s.1, s32[128]{0:T(128)} %dest_s.1, s32[1,128]{1,0:T(1,128)} %bitcast.2, s32[1,128]{1,0:T(1,128)} %bitcast.3, f32[896]{0:T(1024)} %gain.1, bf16[3,2,576]{2,1,0:T(2,128)(2,1)} %fresh_all.1, ...), custom_call_target="tpu_custom_call" | custom-call | tf_op jit(solution)/shard_map/layer/pallas_call | solution.py:628
  123.4 1.5 %copy.16 = bf16[3,16,896]{2,1,0:T(8,128)(2,1)} copy(bf16[3,16,896]{2,1,0:T(8,128)(2,1)} %layer.1) | data formatting | bytes 172032
